TPU v7x, 32 devices: a whole 2x2x4 slice. The times are simulated.
32 devices in a mesh: parts: 2 (over x), gx: 16 (over z, y, core).
Axes of the slice: x: 2, y: 2, z: 4, core: 2. Of those that a mesh axis runs over, the one named last changes fastest.
Arguments:
- features: bfloat16 [16384, 256], P(('parts', 'gx')), parts along dimension 0, may hold values from -6 to 6
- neighbours: int32 [27, 16384], P(None, ('parts', 'gx')), parts along dimension 1, may hold values from 0 to 640, as said below
- rim_rows: int32 [4096], P(('parts', 'gx')), parts along dimension 0, may hold values from 0 to 511, as said below
- tile_slot: int32 [16384], P(('parts', 'gx')), parts along dimension 0, may hold values from 0 to 1023, as said below
- patch_rows: int32 [16384], P(('parts', 'gx')), parts along dimension 0, may hold values from 0 to 1023, as said below
- conv_weight: bfloat16 [6912, 256], replicated, may hold values from -0.078125 to 0.078125
- norm_gain: float32 [256], replicated, may hold values from 0.1 to 1.9
- qkv_weight: bfloat16 [256, 768], replicated
- proj_weight: bfloat16 [256, 256], replicated, may hold values from -0.375 to 0.375
- out_grad: bfloat16 [16384, 256], P(('parts', 'gx')), parts along dimension 0, may hold values from -6 to 6
Outputs:
- block_out: bfloat16 [16384, 256], P(('parts', 'gx')), parts along dimension 0
- conv_grad: float32 [13824, 256], P(('parts', 'gx')), parts along dimension 0
- qkv_grad: float32 [512, 768], P(('parts', 'gx')), parts along dimension 0
- proj_grad: float32 [512, 256], P(('parts', 'gx')), parts along dimension 0
- gain_grad: float32 [512], P(('parts', 'gx')), parts along dimension 0
There are 2 independent parts, one for each index of `parts`. A program takes and returns all parts, laid end to end along the dimension named above; an argument that names none is the same for every part. Nothing has to cross between parts.
Inputs may be any that keep to these rules, and one draw needn't show every extreme that they name: `tile_slot`: value // 64 is the owner tile of the point's patch, value % 64 its slot; a tile's entries are distinct; at most 64 points of one tile go to one patch, exactly 64 for some pair in every draw; every patch receives exactly 512 points. `patch_rows`: A patch's 512 entries are distinct and are exactly the slots t * 64 + s filled for it by the tiles. `neighbours`: rows 0 to 511 of a tile's table are its points, the next 64 come from the previous tile, the next 64 from the next tile; 640 means no neighbour; offset 13 is the point itself. `rim_rows`: per tile 2 * 64 distinct rows: first those sent to the previous tile, then those sent to the next.
All inputs are finite; a program needn't handle non-finite values.
Results may differ from a plain program's by a relative error of at most 0.012.
The roundings to bfloat16 on the way count: a program that leaves them out, or rounds other values in their place, can miss the bound.
Values may be sent and summed in bfloat16 or wider, within the bound.
A program may use at most 128 MiB of HBM per device.

v0:
```python
import jax
import jax.numpy as jnp
from jax import lax
from jax.sharding import PartitionSpec as P

HEADS = 16
HEAD = 16


def extended_2(block, sides, width):
    for axis, dim in sides:
        count = lax.axis_size(axis)
        forward = [(i, i + 1) for i in range(count - 1)]
        backward = [(target, source) for source, target in forward]
        low = lax.ppermute(
            lax.slice_in_dim(block, block.shape[dim] - width, None, axis=dim), axis, forward
        )
        high = lax.ppermute(lax.slice_in_dim(block, 0, width, axis=dim), axis, backward)
        block = jnp.concatenate([low, block, high], axis=dim)
    return block


def softmax_weights(query, keys, scaling):
    scores = jnp.einsum("qhd,khd->hqk", query, keys, preferred_element_type=jnp.float32) * scaling
    highest = jnp.max(scores, axis=-1, keepdims=True)
    raised = jnp.exp(scores - highest)
    return raised / jnp.sum(raised, axis=-1, keepdims=True)


def grouped(values):
    length = values.shape[0]
    return values.reshape(length, HEADS // 4, 4, HEAD).transpose(1, 0, 2, 3)


def ungrouped(values):
    return values.transpose(1, 0, 2, 3).reshape(values.shape[1], -1)


def attend_forward(pieces):
    query, keys, values = pieces
    probs = softmax_weights(query, keys, HEAD ** (-0.5)).astype(jnp.bfloat16)
    return jnp.einsum("hqk,khd->qhd", probs, values, preferred_element_type=jnp.float32).astype(
        jnp.bfloat16
    )


def attend_backward(pieces):
    query, keys, values, upstream = pieces
    scaling = HEAD ** (-0.5)
    probs = softmax_weights(query, keys, scaling)
    grad_vals = jnp.einsum(
        "hqk,qhd->khd", probs.astype(jnp.bfloat16), upstream, preferred_element_type=jnp.float32
    )
    grad_probs = jnp.einsum("qhd,khd->hqk", upstream, values, preferred_element_type=jnp.float32)
    row_total = jnp.sum(grad_probs * probs, axis=-1, keepdims=True)
    grad_scores = (probs * (grad_probs - row_total) * scaling).astype(jnp.bfloat16)
    grad_query = jnp.einsum("hqk,khd->qhd", grad_scores, keys, preferred_element_type=jnp.float32)
    grad_keys = jnp.einsum("hqk,qhd->khd", grad_scores, query, preferred_element_type=jnp.float32)
    return (grad_query, grad_keys, grad_vals)


def patch_forward(patch_in, qkv_weight, proj_weight):
    channels = patch_in.shape[1]
    qkv = jnp.dot(patch_in, qkv_weight, preferred_element_type=jnp.float32).astype(jnp.bfloat16)
    heads_split = (
        grouped(qkv[:, :channels]),
        grouped(qkv[:, channels : 2 * channels]),
        grouped(qkv[:, 2 * channels :]),
    )
    attended = ungrouped(lax.map(attend_forward, heads_split))
    proj_out = jnp.dot(attended, proj_weight, preferred_element_type=jnp.float32).astype(
        jnp.bfloat16
    )
    return (heads_split, attended, proj_out)


def patch_backward(patch_in, patch_grad, heads_split, attended, qkv_weight, proj_weight):
    proj_term = lax.dot_general(
        attended, patch_grad, (((0,), (0,)), ((), ())), preferred_element_type=jnp.float32
    )
    upstream = lax.dot_general(
        patch_grad, proj_weight, (((1,), (1,)), ((), ())), preferred_element_type=jnp.float32
    ).astype(jnp.bfloat16)
    grads = lax.map(
        attend_backward, (heads_split[0], heads_split[1], heads_split[2], grouped(upstream))
    )
    grad_qkv = jnp.concatenate([ungrouped(piece) for piece in grads], axis=1).astype(jnp.bfloat16)
    qkv_term = lax.dot_general(
        patch_in, grad_qkv, (((0,), (0,)), ((), ())), preferred_element_type=jnp.float32
    )
    grad_normed = lax.dot_general(
        grad_qkv, qkv_weight, (((1,), (1,)), ((), ())), preferred_element_type=jnp.float32
    ).astype(jnp.bfloat16)
    return (grad_normed, qkv_term, proj_term)


def on_device(
    features,
    neighbours,
    rim_rows,
    tile_slot,
    patch_rows,
    conv_weight,
    norm_gain,
    qkv_weight,
    proj_weight,
    out_grad,
):
    tile_rows, channels = features.shape
    tile_count = lax.axis_size("gx")
    capacity = 2 * tile_rows // tile_count
    rim_size = rim_rows.shape[0] // 2
    rim_feats = features[rim_rows]
    extended = extended_2(rim_feats, (("gx", 0),), rim_size)
    table = jnp.concatenate(
        [
            features,
            extended[:rim_size],
            extended[3 * rim_size :],
            jnp.zeros((1, channels), jnp.bfloat16),
        ],
        axis=0,
    )
    gathered = table[neighbours.T].reshape(tile_rows, -1)
    hidden = features.astype(jnp.float32) + jnp.dot(
        gathered, conv_weight, preferred_element_type=jnp.float32
    )
    row_mean = jnp.mean(hidden, axis=-1, keepdims=True)
    centred = hidden - row_mean
    inv_std = 1.0 / jnp.sqrt(jnp.mean(centred * centred, axis=-1, keepdims=True) + 1e-05)
    standard = centred * inv_std
    normed = (standard * norm_gain).astype(jnp.bfloat16)

    def to_slots(values):
        return (
            jnp.zeros((tile_count * capacity, channels), values.dtype)
            .at[tile_slot]
            .set(values)
            .reshape(tile_count, capacity, channels)
        )

    def from_patch(values):
        return (
            jnp.zeros((tile_count * capacity, channels), values.dtype)
            .at[patch_rows]
            .set(values)
            .reshape(tile_count, capacity, channels)
        )

    recv_normed, recv_grad = (
        lax.all_to_all(to_slots(normed), "gx", split_axis=0, concat_axis=0, tiled=True),
        lax.all_to_all(to_slots(out_grad), "gx", split_axis=0, concat_axis=0, tiled=True),
    )
    patch_in = recv_normed.reshape(tile_count * capacity, channels)[patch_rows]
    patch_grad = recv_grad.reshape(tile_count * capacity, channels)[patch_rows]
    heads_split, attended, proj_out = patch_forward(patch_in, qkv_weight, proj_weight)
    grad_normed, qkv_term, proj_term = patch_backward(
        patch_in, patch_grad, heads_split, attended, qkv_weight, proj_weight
    )
    returned, grad_recv = (
        lax.all_to_all(from_patch(proj_out), "gx", split_axis=0, concat_axis=0, tiled=True),
        lax.all_to_all(from_patch(grad_normed), "gx", split_axis=0, concat_axis=0, tiled=True),
    )
    returned_rows = returned.reshape(tile_count * capacity, channels)[tile_slot]
    block_out = (hidden + returned_rows.astype(jnp.float32)).astype(jnp.bfloat16)
    grad_back = grad_recv.reshape(tile_count * capacity, channels)[tile_slot].astype(jnp.float32)
    gain_term = jnp.sum(grad_back * standard, axis=0)
    scaled = grad_back * norm_gain
    grad_hidden = out_grad.astype(jnp.float32) + inv_std * (
        scaled
        - jnp.mean(scaled, axis=-1, keepdims=True)
        - standard * jnp.mean(scaled * standard, axis=-1, keepdims=True)
    )
    grad_hidden = grad_hidden.astype(jnp.bfloat16)
    conv_grad = lax.psum_scatter(
        lax.dot_general(
            gathered, grad_hidden, (((0,), (0,)), ((), ())), preferred_element_type=jnp.float32
        ),
        "gx",
        scatter_dimension=0,
        tiled=True,
    )
    qkv_grad, proj_grad, gain_grad = (
        lax.psum_scatter(qkv_term, "gx", scatter_dimension=0, tiled=True),
        lax.psum_scatter(proj_term, "gx", scatter_dimension=0, tiled=True),
        lax.psum_scatter(gain_term, "gx", scatter_dimension=0, tiled=True),
    )
    return (block_out, conv_grad, qkv_grad, proj_grad, gain_grad)


def solution(mesh):
    placed = (
        P(("parts", "gx"), None),
        P(None, ("parts", "gx")),
        P(("parts", "gx")),
        P(("parts", "gx")),
        P(("parts", "gx")),
        P(),
        P(),
        P(),
        P(),
        P(("parts", "gx"), None),
    )
    return jax.shard_map(
        on_device,
        mesh=mesh,
        in_specs=placed,
        out_specs=(
            P(("parts", "gx"), None),
            P(("parts", "gx"), None),
            P(("parts", "gx"), None),
            P(("parts", "gx"), None),
            P(("parts", "gx")),
        ),
        check_vma=False,
    )
```

profile of v0, /device:TPU:13, one launch (start us, length us, event | category | flops | bytes accessed | tf_op | source)
XLA Modules:
  0.0 519.7 jit_solution(11792516260531387212)
XLA Ops:
  11.9 3.7 collective-permute-start
  21.8 6.5 %all-to-all-start.2 = ((bf16[16,64,256]{2,1,0:T(8,128)(2,1)}), bf16[16,64,256]{2,1,0:T(8,128)(2,1)}, u32[]{:S(2)}, u32[]{:S(2)}) async-start(bf16[16,64,256]{2,1,0:T(8,128)(2,1)} %bitcast.166), calls=%async_computation.2 | async-start | bytes 1048576 | tf_op jit(solution)/shard_map/all_to_all | solution.py:152
  38.4 34.9 %gather_fusion.1 = bf16[13824,256]{1,0:T(8,128)(2,1)} fusion(bf16[641,256]{1,0:T(8,128)(2,1)} %maximum_maximum_fusion, s32[14336]{0:T(1024)} %pad_clamp_fusion), kind=kCustom, calls=%fused_computation.1 | custom fusion | bytes 14211072 | tf_op jit(solution)/shard_map/gather | solution.py:124
  73.3 13.8 %reshape.91 = bf16[512,6912]{1,0:T(8,128)(2,1)} reshape(bf16[13824,256]{1,0:T(8,128)(2,1)} %gather_fusion.1) | data formatting | bytes 14155776 | tf_op jit(solution)/shard_map/reshape | solution.py:124
  87.0 5.1 fusion.167
  99.1 6.0 %all-to-all-start = ((bf16[16,64,256]{2,1,0:T(8,128)(2,1)}), bf16[16,64,256]{2,1,0:T(8,128)(2,1)}, u32[]{:S(2)}, u32[]{:S(2)}) async-start(bf16[16,64,256]{2,1,0:T(8,128)(2,1)} %bitcast.167), calls=%async_computation | async-start | bytes 1048576 | tf_op jit(solution)/shard_map/all_to_all | solution.py:151
  111.7 7.1 %all-to-all-done = bf16[16,64,256]{2,1,0:T(8,128)(2,1)} async-done(((bf16[16,64,256]{2,1,0:T(8,128)(2,1)}), bf16[16,64,256]{2,1,0:T(8,128)(2,1)}, u32[]{:S(2)}, u32[]{:S(2)}) %all-to-all-start) | async-done | bytes 524320 | tf_op jit(solution)/shard_map/all_to_all | solution.py:151
  129.8 113.4 %while.25 = (s32[]{:T(128)}, bf16[4,512,4,16]{1,3,2,0:T(8,128)(2,1)}, bf16[4,512,4,16]{1,3,2,0:T(8,128)(2,1)}, bf16[4,512,4,16]{1,3,2,0:T(8,128)(2,1)}, bf16[4,5...) while((s32[]{:T(128)}, ...), condition=%wide.region_13.14_spmd, body=%wide.region_9.13_spmd.sunk | while | flops 187700736 | bytes 47043676 | solution.py:84
  129.8 5.0 fusion.218
  138.5 8.0 %fusion.220 = bf16[4,512,4,16]{1,3,2,0:T(8,128)(2,1)} fusion(bf16[4,512,4,16]{1,3,2,0:T(8,128)(2,1)} %get-tuple-element.237, s32[]{:T(128)} %get-tuple-element.235, f32[4,512,512]{1,2,0:T(8,128)} %fusion.217, bf16[4,512,4,16]{1,3,2,0:T(8,128)(2,1)} %get-tuple-element.249, f32[4,512,512]{1,2,0:T(8,128)} %get-tuple-element.224, ...), kind=kOutput, calls=%fused_computation.55.clone.1 | convolution fusion | flops 40897024 | bytes 16991232 | tf_op jit(solution)/shard_map/while/body/eval_jaxpr/hqk,qhd->khd/dot_general | solution.py:58
  150.0 8.2 %fusion.219 = bf16[4,512,4,16]{1,3,2,0:T(8,128)(2,1)} fusion(bf16[4,512,4,16]{1,3,2,0:T(8,128)(2,1)} %get-tuple-element.236, s32[]{:T(128)} %get-tuple-element.235, f32[4,512,512]{1,2,0:T(8,128)} %fusion.217, bf16[4,512,4,16]{1,3,2,0:T(8,128)(2,1)} %get-tuple-element.248, f32[4,512,512]{1,2,0:T(8,128)} %get-tuple-element.224, ...), kind=kOutput, calls=%fused_computation.53.clone.1 | convolution fusion | flops 40897024 | bytes 16991232 | tf_op jit(solution)/shard_map/while/body/eval_jaxpr/hqk,khd->qhd/dot_general | solution.py:57
  158.2 5.0 fusion.218
  166.9 8.0 %fusion.220 = bf16[4,512,4,16]{1,3,2,0:T(8,128)(2,1)} fusion(bf16[4,512,4,16]{1,3,2,0:T(8,128)(2,1)} %get-tuple-element.237, s32[]{:T(128)} %get-tuple-element.235, f32[4,512,512]{1,2,0:T(8,128)} %fusion.217, bf16[4,512,4,16]{1,3,2,0:T(8,128)(2,1)} %get-tuple-element.249, f32[4,512,512]{1,2,0:T(8,128)} %get-tuple-element.224, ...), kind=kOutput, calls=%fused_computation.55.clone.1 | convolution fusion | flops 40897024 | bytes 16991232 | tf_op jit(solution)/shard_map/while/body/eval_jaxpr/hqk,qhd->khd/dot_general | solution.py:58
  178.3 8.2 %fusion.219 = bf16[4,512,4,16]{1,3,2,0:T(8,128)(2,1)} fusion(bf16[4,512,4,16]{1,3,2,0:T(8,128)(2,1)} %get-tuple-element.236, s32[]{:T(128)} %get-tuple-element.235, f32[4,512,512]{1,2,0:T(8,128)} %fusion.217, bf16[4,512,4,16]{1,3,2,0:T(8,128)(2,1)} %get-tuple-element.248, f32[4,512,512]{1,2,0:T(8,128)} %get-tuple-element.224, ...), kind=kOutput, calls=%fused_computation.53.clone.1 | convolution fusion | flops 40897024 | bytes 16991232 | tf_op jit(solution)/shard_map/while/body/eval_jaxpr/hqk,khd->qhd/dot_general | solution.py:57
  186.6 5.0 fusion.218
  191.5 3.7 fusion.217
  195.2 8.0 %fusion.220 = bf16[4,512,4,16]{1,3,2,0:T(8,128)(2,1)} fusion(bf16[4,512,4,16]{1,3,2,0:T(8,128)(2,1)} %get-tuple-element.237, s32[]{:T(128)} %get-tuple-element.235, f32[4,512,512]{1,2,0:T(8,128)} %fusion.217, bf16[4,512,4,16]{1,3,2,0:T(8,128)(2,1)} %get-tuple-element.249, f32[4,512,512]{1,2,0:T(8,128)} %get-tuple-element.224, ...), kind=kOutput, calls=%fused_computation.55.clone.1 | convolution fusion | flops 40897024 | bytes 16991232 | tf_op jit(solution)/shard_map/while/body/eval_jaxpr/hqk,qhd->khd/dot_general | solution.py:58
  206.7 8.2 %fusion.219 = bf16[4,512,4,16]{1,3,2,0:T(8,128)(2,1)} fusion(bf16[4,512,4,16]{1,3,2,0:T(8,128)(2,1)} %get-tuple-element.236, s32[]{:T(128)} %get-tuple-element.235, f32[4,512,512]{1,2,0:T(8,128)} %fusion.217, bf16[4,512,4,16]{1,3,2,0:T(8,128)(2,1)} %get-tuple-element.248, f32[4,512,512]{1,2,0:T(8,128)} %get-tuple-element.224, ...), kind=kOutput, calls=%fused_computation.53.clone.1 | convolution fusion | flops 40897024 | bytes 16991232 | tf_op jit(solution)/shard_map/while/body/eval_jaxpr/hqk,khd->qhd/dot_general | solution.py:57
  214.9 5.0 fusion.218
  223.6 8.0 %fusion.220 = bf16[4,512,4,16]{1,3,2,0:T(8,128)(2,1)} fusion(bf16[4,512,4,16]{1,3,2,0:T(8,128)(2,1)} %get-tuple-element.237, s32[]{:T(128)} %get-tuple-element.235, f32[4,512,512]{1,2,0:T(8,128)} %fusion.217, bf16[4,512,4,16]{1,3,2,0:T(8,128)(2,1)} %get-tuple-element.249, f32[4,512,512]{1,2,0:T(8,128)} %get-tuple-element.224, ...), kind=kOutput, calls=%fused_computation.55.clone.1 | convolution fusion | flops 40897024 | bytes 16991232 | tf_op jit(solution)/shard_map/while/body/eval_jaxpr/hqk,qhd->khd/dot_general | solution.py:58
  235.0 8.2 %fusion.219 = bf16[4,512,4,16]{1,3,2,0:T(8,128)(2,1)} fusion(bf16[4,512,4,16]{1,3,2,0:T(8,128)(2,1)} %get-tuple-element.236, s32[]{:T(128)} %get-tuple-element.235, f32[4,512,512]{1,2,0:T(8,128)} %fusion.217, bf16[4,512,4,16]{1,3,2,0:T(8,128)(2,1)} %get-tuple-element.248, f32[4,512,512]{1,2,0:T(8,128)} %get-tuple-element.224, ...), kind=kOutput, calls=%fused_computation.53.clone.1 | convolution fusion | flops 40897024 | bytes 16991232 | tf_op jit(solution)/shard_map/while/body/eval_jaxpr/hqk,khd->qhd/dot_general | solution.py:57
  249.2 5.0 all-to-all-start.3
  254.2 32.8 %while.24 = (s32[]{:T(128)}, bf16[4,512,4,16]{1,3,2,0:T(8,128)(2,1)}, bf16[4,512,4,16]{1,3,2,0:T(8,128)(2,1)}, bf16[4,512,4,16]{1,3,2,0:T(8,128)(2,1)}, bf16[4,512,4,16]{1,3,2,0:T(8,128)(2,1)}, /*index=5*/s32[]{:T(128)}) while((s32[]{:T(128)}, bf16[4,512,4,16]{1,3,2,0:T(8,128)(2,1)}, bf16[4,512,4,16]{1,3,2,0:T(8,128)(2,1)}, ...), condition=%wide.region_6.0_spmd, body=%wide.region_3.6_spmd.sunk | while | flops 72385024 | bytes 8669253 | solution.py:70
  254.2 5.0 fusion.205
  262.4 5.0 fusion.205
  270.6 5.0 fusion.205
  278.8 5.0 fusion.205
  292.4 6.1 %all-to-all-start.1 = ((bf16[16,64,256]{2,1,0:T(8,128)(2,1)}), bf16[16,64,256]{2,1,0:T(8,128)(2,1)}, u32[]{:S(2)}, u32[]{:S(2)}) async-start(bf16[16,64,256]{2,1,0:T(8,128)(2,1)} %bitcast.165), calls=%async_computation.1 | async-start | bytes 1048576 | tf_op jit(solution)/shard_map/all_to_all | solution.py:161
  320.1 8.4 %fusion.130 = f32[6912,256]{1,0:T(8,128)} fusion(bf16[512,6912]{1,0:T(8,128)(2,1)} %reshape.91, bf16[512,256]{0,1:T(8,128)(2,1)} %copy.53, bf16[512,256]{0,1:T(8,128)(2,1)} %copy.52, f32[512,256]{0,1:T(8,128)} %copy-done.1, f32[512]{0:T(512)S(1)} %get-tuple-element.136, f32[512]{0:T(512)S(1)} %get-tuple-element.137, f32[256]{0:T(256)S(1)} %copy-done.2, ...), kind=kOutput, calls=%fused_computation.113 | convolution fusion | flops 1813381120 | bytes 15213568 | tf_op jit(solution)/shard_map/dot_general | solution.py:176
  332.2 22.1 %all-reduce = f32[256]{0:T(256)S(1)} all-reduce(f32[256]{0:T(256)S(1)} %copy-done.5), channel_id=5, replica_groups=mesh['parts'=2,'gx'=16] {'gx'}, use_global_device_ids=true, to_apply=%region_21.22.clone | all-reduce | flops 256 | bytes 2048
  357.0 60.0 %reduce-scatter.6.cloned.1.call-done = f32[16,768]{1,0:T(8,128)} async-done(((f32[256,768]{1,0:T(8,128)}), f32[16,768]{1,0:T(8,128)}) %reduce-scatter.6.cloned.1.call-update) | async-done | bytes 49168 | tf_op jit(solution)/shard_map/reduce_scatter | solution.py:184
  417.0 96.2 %reduce-scatter.4.cloned.1.call-done = f32[432,256]{1,0:T(8,128)} async-done(((f32[6912,256]{1,0:T(8,128)}), f32[432,256]{1,0:T(8,128)}) %reduce-scatter.4.cloned.1.call-update) | async-done | bytes 442384 | tf_op jit(solution)/shard_map/reduce_scatter | solution.py:175
  (88 shorter events, 121.9 us)
Async XLA Ops:
  7.2 79.9 %copy-start = (bf16[6912,256]{1,0:T(8,128)(2,1)S(1)}, bf16[6912,256]{1,0:T(8,128)(2,1)}, u32[]{:S(2)}) copy-start(bf16[6912,256]{1,0:T(8,128)(2,1)} %param.19) | copy-start | bytes 10616836
  11.9 24.6 %collective-permute-start = (bf16[64,256]{1,0:T(8,128)(2,1)}, bf16[64,256]{1,0:T(8,128)(2,1)}, u32[]{:S(2)}, u32[]{:S(2)}) collective-permute-start(bf16[64,256]{1,0:T(8,128)(2,1)} %get-tuple-element.132), channel_id=1, source_target_pairs={{0,1},{1,2},{2,3},{3,4},{4,5},{5,6},{6,7},{7,8},{8,9},{9,10},{10,1... | collective-permute-start | bytes 98312 | tf_op jit(solution)/shard_map/ppermute | solution.py:15
  15.6 20.9 %collective-permute-start.1 = (bf16[64,256]{1,0:T(8,128)(2,1)}, bf16[64,256]{1,0:T(8,128)(2,1)}, u32[]{:S(2)}, u32[]{:S(2)}) collective-permute-start(bf16[64,256]{1,0:T(8,128)(2,1)} %get-tuple-element.133), channel_id=1, source_target_pairs={{1,0},{2,1},{3,2},{4,3},{5,4},{6,5},{7,6},{8,7},{9,8},{10,9},{11,1... | collective-permute-start | bytes 98312 | tf_op jit(solution)/shard_map/ppermute | solution.py:18
  18.3 55.0 %copy-start.3 = (s32[512]{0:T(512)}, s32[512]{0:T(512)S(1)}, u32[]{:S(2)}) copy-start(s32[512]{0:T(512)S(1)} %compare_select_fusion.1) | copy-start | bytes 6148
  21.8 77.3 %all-to-all-start.2 = ((bf16[16,64,256]{2,1,0:T(8,128)(2,1)}), bf16[16,64,256]{2,1,0:T(8,128)(2,1)}, u32[]{:S(2)}, u32[]{:S(2)}) async-start(bf16[16,64,256]{2,1,0:T(8,128)(2,1)} %bitcast.166), calls=%async_computation.2 | async-start | bytes 1048576 | tf_op jit(solution)/shard_map/all_to_all | solution.py:152
  87.0 5.9 %copy-start.2 = (f32[256]{0:T(256)S(1)}, f32[256]{0:T(256)}, u32[]{:S(2)}) copy-start(f32[256]{0:T(256)} %param.20) | copy-start | bytes 3076
  92.1 0.8 copy-start.1
  99.1 19.7 %all-to-all-start = ((bf16[16,64,256]{2,1,0:T(8,128)(2,1)}), bf16[16,64,256]{2,1,0:T(8,128)(2,1)}, u32[]{:S(2)}, u32[]{:S(2)}) async-start(bf16[16,64,256]{2,1,0:T(8,128)(2,1)} %bitcast.167), calls=%async_computation | async-start | bytes 1048576 | tf_op jit(solution)/shard_map/all_to_all | solution.py:151
  105.8 0.6 copy-start.4
  249.2 43.3 %all-to-all-start.3 = ((bf16[16,64,256]{2,1,0:T(8,128)(2,1)}), bf16[16,64,256]{2,1,0:T(8,128)(2,1)}, u32[]{:S(2)}, u32[]{:S(2)}) async-start(bf16[16,64,256]{2,1,0:T(8,128)(2,1)} %bitcast.164), calls=%async_computation.3 | async-start | bytes 1048576 | tf_op jit(solution)/shard_map/all_to_all | solution.py:162
  292.4 19.8 %all-to-all-start.1 = ((bf16[16,64,256]{2,1,0:T(8,128)(2,1)}), bf16[16,64,256]{2,1,0:T(8,128)(2,1)}, u32[]{:S(2)}, u32[]{:S(2)}) async-start(bf16[16,64,256]{2,1,0:T(8,128)(2,1)} %bitcast.165), calls=%async_computation.1 | async-start | bytes 1048576 | tf_op jit(solution)/shard_map/all_to_all | solution.py:161
  298.5 58.5 %reduce-scatter.8.cloned.1.call-start = ((), (), s32[]{:S(2)}) async-start(), calls=%async_computation.9 | async-start | bytes 278528 | tf_op jit(solution)/shard_map/reduce_scatter | solution.py:185
  300.6 116.4 %reduce-scatter.6.cloned.1.call-start = ((), (), s32[]{:S(2)}) async-start(), calls=%async_computation.8 | async-start | bytes 835584 | tf_op jit(solution)/shard_map/reduce_scatter | solution.py:184
  304.9 208.2 %reduce-scatter.4.cloned.1.call-start = ((), (), s32[]{:S(2)}) async-start(), calls=%async_computation.7 | async-start | bytes 7520256 | tf_op jit(solution)/shard_map/reduce_scatter | solution.py:175
  328.5 0.7 copy-start.6
  328.5 3.7 copy-start.5
Sparse Core Ops, SparseCore 0:
  303.4 53.5 reduce-scatter.7
  361.1 55.7 reduce-scatter.5
  422.1 90.9 reduce-scatter.3
where the time goes:
time: 525 us; the launch traced here: 520 us
  matrix products  172 us (33%)
  waiting for transfers between devices  167 us (32%)
  local copies, waits for them, and re-layouts  104 us (20%)
  starting transfers between devices  29.3 us (6%)
  blocking collectives  22.1 us (4%)
  between operations  14.5 us (3%)
  other arithmetic  11.3 us (2%)
    reduce_scatter x1, waiting for transfers between devices, on_device(): lax.psum_scatter(lax.dot_general(gathered, grad_hidden, (((0,), (0,)), ((...  96.2 us
    reduce_scatter x1, waiting for transfers between devices, on_device(): lax.psum_scatter(qkv_term, 'gx', scatter_dimension=0, tiled=True)  60 us
    sub x8, matrix products, softmax_weights(): raised = jnp.exp(scores - highest)  39.9 us
    gather x1, local copies, waits for them, and re-layouts, on_device(): gathered = table[neighbours.T].reshape(tile_rows, -1)  34.9 us
    dot_general x4, matrix products, attend_backward(): jnp.einsum('hqk,khd->qhd', grad_scores, keys, preferred_element_type=jnp....  32.9 us
    dot_general x4, matrix products, attend_backward(): jnp.einsum('hqk,qhd->khd', grad_scores, query, preferred_element_type=jnp...  31.9 us
    unnamed x1, blocking collectives  22.1 us
    dot_general x4, matrix products, attend_backward(): jnp.einsum('qhd,khd->hqk', upstream, values, preferred_element_type=jnp.f...  14.7 us
  transfers between devices with their start and end apart: 9, of which 5 were waited for; matrix products, arithmetic and copies ran while one was open for 29% of the time, Pallas kernels for 0%

commit v1 on v0

v1 whole, which is shorter than its diff:
```python
import functools

import jax
import jax.numpy as jnp
from jax import lax
from jax.experimental import pallas as pl
from jax.experimental.pallas import tpu as pltpu
from jax.sharding import PartitionSpec as P

HEADS = 16
HEAD = 16
LIMIT = 56 * 1024 * 1024
F32 = jnp.float32
BF16 = jnp.bfloat16
VMEM = pl.BlockSpec(memory_space=pltpu.VMEM)


def dot(a, b, ca=1, cb=0):
    return lax.dot_general(a, b, (((ca,), (cb,)), ((), ())), preferred_element_type=F32)


def hot_rows(index_row, count):
    rows = lax.broadcasted_iota(jnp.int32, (count, index_row.shape[1]), 0)
    return jnp.where(rows == index_row, 1.0, 0.0).astype(BF16)


def hot_columns(index_column, count):
    columns = lax.broadcasted_iota(jnp.int32, (index_column.shape[0], count), 1)
    return jnp.where(columns == index_column, 1.0, 0.0).astype(BF16)


def normalise(hidden):
    centred = hidden - jnp.mean(hidden, axis=-1, keepdims=True)
    inv_std = 1.0 / jnp.sqrt(jnp.mean(centred * centred, axis=-1, keepdims=True) + 1e-05)
    return centred * inv_std, inv_std


def start_kernel(feats, grads, rim_col, slot_row, rim_out, slots_out):
    rim_out[...] = dot(hot_columns(rim_col[...], feats.shape[0]), feats[...]).astype(BF16)
    slots_out[...] = dot(hot_rows(slot_row[...], slots_out.shape[0]), grads[...]).astype(BF16)


def conv_kernel(
    feats, low, high, nbrs, weight, gain, slot_row, gathered_out, hidden_out, slots_out, table, acc
):
    k = pl.program_id(0)
    rows = feats.shape[0]
    rim = low.shape[0]

    @pl.when(k == 0)
    def _():
        table[:, :rows] = feats[...].T
        table[:, rows : rows + rim] = low[...].T
        table[:, rows + rim :] = high[...].T
        acc[...] = jnp.zeros_like(acc)

    gathered = dot(table[...], hot_rows(nbrs[0], rows + 2 * rim)).astype(BF16)
    gathered_out[0] = gathered
    acc[...] += dot(weight[...], gathered, 0, 0)

    @pl.when(k == pl.num_programs(0) - 1)
    def _():
        hidden = feats[...].astype(F32) + acc[...].T
        hidden_out[...] = hidden
        standard, _ = normalise(hidden)
        normed = (standard * gain[...]).astype(BF16)
        slots_out[...] = dot(hot_rows(slot_row[...], slots_out.shape[0]), normed).astype(BF16)


def attention_kernel(
    recv_normed, recv_grad, rows_row, rows_col, qkv_w, proj_w,
    out_proj, out_grad, qkv_term, proj_term,
    qkv_t, scaled_t, up_t, att_t, grad_t,
):
    channels = proj_w.shape[0]
    slots = recv_normed.shape[0]
    picks = hot_columns(rows_col[...], slots)
    patch_in = dot(picks, recv_normed[...]).astype(BF16)
    patch_grad = dot(picks, recv_grad[...]).astype(BF16)
    qkv = dot(patch_in, qkv_w[...]).T
    qkv_t[...] = qkv.astype(BF16)
    scaled_t[...] = (qkv_t[:channels, :].astype(F32) * 0.25).astype(BF16)
    up_t[...] = dot(patch_grad, proj_w[...], 1, 1).T.astype(BF16)

    def head(h, carry):
        def part(ref, base=0):
            return ref[pl.ds(pl.multiple_of(base + h * HEAD, HEAD), HEAD), :]

        query, keys, values = part(qkv_t), part(qkv_t, channels), part(qkv_t, 2 * channels)
        query_low = part(scaled_t)
        up = part(up_t)
        up_low = (up.astype(F32) * 0.25).astype(BF16)
        scores = dot(keys, query_low, 0, 0)
        raised = jnp.exp(scores - jnp.max(scores, axis=0, keepdims=True))
        probs = raised * (1.0 / jnp.sum(raised, axis=0, keepdims=True))
        probs_low = probs.astype(BF16)
        grad_probs = dot(values, up_low, 0, 0)
        total = jnp.sum(grad_probs * probs, axis=0, keepdims=True)
        grad_scores = (probs * (grad_probs - total)).astype(BF16)

        def put(ref, value, base=0):
            ref[pl.ds(pl.multiple_of(base + h * HEAD, HEAD), HEAD), :] = value.astype(BF16)

        put(att_t, dot(values, probs_low))
        put(grad_t, dot(up, probs_low, 1, 1), 2 * channels)
        put(grad_t, dot(keys, grad_scores))
        put(grad_t, dot(query, grad_scores, 1, 1), channels)
        return carry

    lax.fori_loop(0, HEADS, head, 0, unroll=2)
    back = hot_rows(rows_row[...], slots)
    proj_out = dot(att_t[...], proj_w[...], 0, 0).astype(BF16)
    out_proj[...] = dot(back, proj_out).astype(BF16)
    proj_term[...] = dot(att_t[...], patch_grad)
    grad_qkv = grad_t[...].astype(F32).T.astype(BF16)
    qkv_term[...] = dot(patch_in, grad_qkv, 0, 0)
    grad_normed = dot(grad_qkv, qkv_w[...], 1, 1).astype(BF16)
    out_grad[...] = dot(back, grad_normed).astype(BF16)


def backward_kernel(
    hidden, back_proj, back_grad, out_grad, gain, slot_col, gathered,
    block_out, gain_term, conv_term, grad_hidden,
):
    @pl.when(pl.program_id(0) == 0)
    def _():
        picks = hot_columns(slot_col[...], back_proj.shape[0])
        value = hidden[...]
        block_out[...] = (value + dot(picks, back_proj[...])).astype(BF16)
        grad_back = dot(picks, back_grad[...])
        standard, inv_std = normalise(value)
        gain_term[...] = jnp.sum(grad_back * standard, axis=0, keepdims=True)
        scaled = grad_back * gain[...]
        grad_hidden[...] = (
            out_grad[...].astype(F32)
            + inv_std
            * (
                scaled
                - jnp.mean(scaled, axis=-1, keepdims=True)
                - standard * jnp.mean(scaled * standard, axis=-1, keepdims=True)
            )
        ).astype(BF16)

    conv_term[...] = dot(gathered[0], grad_hidden[...])


def reduce_kernel(
    count, conv, small, conv_out, small_out,
    near_conv, near_small, send_conv, send_small, far_conv, far_small,
    near_send, near_recv, far_send, far_recv,
):
    me = lax.axis_index("gx")
    core = lax.rem(me, 2)
    chip = me // 2
    chips = count // 2
    sibling = chip * 2 + 1 - core
    order = [lax.rem(chip + step, chips) for step in range(1, chips + 1)]
    barrier = pltpu.get_barrier_semaphore()
    pl.semaphore_signal(
        barrier, inc=1, device_id={"gx": sibling}, device_id_type=pl.DeviceIdType.MESH
    )
    for peer in order[:-1]:
        pl.semaphore_signal(
            barrier, inc=1, device_id={"gx": peer * 2 + core}, device_id_type=pl.DeviceIdType.MESH
        )
    pl.semaphore_wait(barrier, chips)

    def copy(source, target, send, recv, device):
        return pltpu.make_async_remote_copy(
            src_ref=source,
            dst_ref=target,
            send_sem=send,
            recv_sem=recv,
            device_id={"gx": device},
            device_id_type=pl.DeviceIdType.MESH,
        )

    near = []
    for step, peer in enumerate(order):
        theirs = peer * 2 + 1 - core
        near.append(
            (
                copy(conv.at[theirs], near_conv.at[step], near_send.at[2 * step],
                     near_recv.at[2 * step], sibling),
                copy(small.at[theirs], near_small.at[step], near_send.at[2 * step + 1],
                     near_recv.at[2 * step + 1], sibling),
            )
        )
        for one in near[-1]:
            one.start()
    far = []
    for step, peer in enumerate(order):
        mine = peer * 2 + core
        for one in near[step]:
            one.wait_recv()
        conv_sum = conv[mine] + near_conv[step]
        small_sum = small[mine] + near_small[step]
        if step < chips - 1:
            send_conv[step] = conv_sum.astype(BF16)
            send_small[step] = small_sum.astype(BF16)
            far.append(
                (
                    copy(send_conv.at[step], far_conv.at[step], far_send.at[2 * step],
                         far_recv.at[2 * step], mine),
                    copy(send_small.at[step], far_small.at[step], far_send.at[2 * step + 1],
                         far_recv.at[2 * step + 1], mine),
                )
            )
            for one in far[-1]:
                one.start()
        else:
            conv_out[...] = conv_sum
            small_out[...] = small_sum
    for step in range(chips - 1):
        for one in far[step]:
            one.wait_recv()
        conv_out[...] += far_conv[step].astype(F32)
        small_out[...] += far_small[step].astype(F32)
    for pair in near:
        for one in pair:
            one.wait_send()
    for pair in far:
        for one in pair:
            one.wait_send()


def params(**more):
    return pltpu.CompilerParams(vmem_limit_bytes=LIMIT, **more)


def shape(dims, dtype):
    return jax.ShapeDtypeStruct(dims, dtype)


def on_device(
    features,
    neighbours,
    rim_rows,
    tile_slot,
    patch_rows,
    conv_weight,
    norm_gain,
    qkv_weight,
    proj_weight,
    out_grad,
):
    rows, channels = features.shape
    count = lax.axis_size("gx")
    capacity = 2 * rows // count
    slots = count * capacity
    rim = rim_rows.shape[0] // 2
    kernel = neighbours.shape[0]
    gain = norm_gain.reshape(1, channels)
    slot_row, slot_col = tile_slot.reshape(1, rows), tile_slot.reshape(rows, 1)
    rows_row, rows_col = patch_rows.reshape(1, rows), patch_rows.reshape(rows, 1)

    rim_feats, grad_slots = pl.pallas_call(
        start_kernel,
        out_shape=(shape((2 * rim, channels), BF16), shape((slots, channels), BF16)),
        in_specs=[VMEM] * 4,
        out_specs=(VMEM, VMEM),
        compiler_params=params(),
        name="start",
    )(features, out_grad, rim_rows.reshape(2 * rim, 1), slot_row)
    forward = [(i, i + 1) for i in range(count - 1)]
    backward = [(target, source) for source, target in forward]
    low = lax.ppermute(rim_feats[rim:], "gx", forward)
    high = lax.ppermute(rim_feats[:rim], "gx", backward)

    def swap(values):
        return lax.all_to_all(
            values.reshape(count, capacity, -1), "gx", split_axis=0, concat_axis=0, tiled=True
        ).reshape(slots, -1)

    recv_grad = swap(grad_slots)

    def full(*dims):
        return pl.BlockSpec(dims, lambda k: (0,) * len(dims))

    gathered, hidden, normed_slots = pl.pallas_call(
        conv_kernel,
        grid=(kernel,),
        out_shape=(
            shape((kernel, channels, rows), BF16),
            shape((rows, channels), F32),
            shape((slots, channels), BF16),
        ),
        in_specs=[
            full(rows, channels),
            full(rim, channels),
            full(rim, channels),
            pl.BlockSpec((1, 1, rows), lambda k: (k, 0, 0)),
            pl.BlockSpec((channels, channels), lambda k: (k, 0)),
            full(1, channels),
            full(1, rows),
        ],
        out_specs=(
            pl.BlockSpec((1, channels, rows), lambda k: (k, 0, 0)),
            full(rows, channels),
            full(slots, channels),
        ),
        scratch_shapes=[
            pltpu.VMEM((channels, rows + 2 * rim), BF16),
            pltpu.VMEM((channels, rows), F32),
        ],
        compiler_params=params(),
        name="conv",
    )(features, low, high, neighbours.reshape(kernel, 1, rows), conv_weight, gain, slot_row)
    recv_normed = swap(normed_slots)

    proj_slots, grad_normed_slots, qkv_term, proj_term = pl.pallas_call(
        attention_kernel,
        out_shape=(
            shape((slots, channels), BF16),
            shape((slots, channels), BF16),
            shape((channels, 3 * channels), F32),
            shape((channels, channels), F32),
        ),
        in_specs=[VMEM] * 6,
        out_specs=(VMEM,) * 4,
        scratch_shapes=[
            pltpu.VMEM((3 * channels, rows), BF16),
            pltpu.VMEM((channels, rows), BF16),
            pltpu.VMEM((channels, rows), BF16),
            pltpu.VMEM((channels, rows), BF16),
            pltpu.VMEM((3 * channels, rows), BF16),
        ],
        compiler_params=params(),
        name="attention",
    )(recv_normed, recv_grad, rows_row, rows_col, qkv_weight, proj_weight)

    back_grad = swap(grad_normed_slots)
    back_proj = swap(proj_slots)

    block_out, gain_term, conv_term = pl.pallas_call(
        backward_kernel,
        grid=(kernel,),
        out_shape=(
            shape((rows, channels), BF16),
            shape((1, channels), F32),
            shape((kernel * channels, channels), F32),
        ),
        in_specs=[
            full(rows, channels),
            full(slots, channels),
            full(slots, channels),
            full(rows, channels),
            full(1, channels),
            full(rows, 1),
            pl.BlockSpec((1, channels, rows), lambda k: (k, 0, 0)),
        ],
        out_specs=(
            full(rows, channels),
            full(1, channels),
            pl.BlockSpec((channels, channels), lambda k: (k, 0)),
        ),
        scratch_shapes=[pltpu.VMEM((rows, channels), BF16)],
        compiler_params=params(),
        name="backward",
    )(hidden, back_proj, back_grad, out_grad, gain, slot_col, gathered)

    conv_rows = kernel * channels // count
    one = channels // count
    used = 4 * one + 1
    small_rows = -(-used // 16) * 16
    small = jnp.concatenate(
        [
            qkv_term.reshape(count, 3 * one, channels),
            proj_term.reshape(count, one, channels),
            jnp.pad(
                gain_term.reshape(count, 1, one),
                ((0, 0), (0, small_rows - used), (0, channels - one)),
            ),
        ],
        axis=1,
    )
    small = jnp.pad(small, ((0, 0), (0, small_rows - small.shape[1]), (0, 0)))
    chips = count // 2
    conv_rows_pad = -(-conv_rows // 16) * 16
    conv_term = conv_term.reshape(count, conv_rows, channels)
    if conv_rows_pad > conv_rows:
        conv_term = jnp.pad(conv_term, ((0, 0), (0, conv_rows_pad - conv_rows), (0, 0)))
    conv_grad, small_sum = pl.pallas_call(
        functools.partial(reduce_kernel, count),
        out_shape=(shape((conv_rows_pad, channels), F32), shape((small_rows, channels), F32)),
        in_specs=[VMEM] * 2,
        out_specs=(VMEM, VMEM),
        scratch_shapes=[
            pltpu.VMEM((chips, conv_rows_pad, channels), F32),
            pltpu.VMEM((chips, small_rows, channels), F32),
            pltpu.VMEM((chips - 1, conv_rows_pad, channels), BF16),
            pltpu.VMEM((chips - 1, small_rows, channels), BF16),
            pltpu.VMEM((chips - 1, conv_rows_pad, channels), BF16),
            pltpu.VMEM((chips - 1, small_rows, channels), BF16),
            pltpu.SemaphoreType.DMA((2 * chips,)),
            pltpu.SemaphoreType.DMA((2 * chips,)),
            pltpu.SemaphoreType.DMA((2 * chips,)),
            pltpu.SemaphoreType.DMA((2 * chips,)),
        ],
        compiler_params=params(collective_id=1, has_side_effects=True),
        name="reduce",
    )(conv_term, small)
    return (
        block_out,
        conv_grad[:conv_rows],
        small_sum[: 3 * one].reshape(one, 3 * channels),
        small_sum[3 * one : 4 * one],
        small_sum[4 * one, :one],
    )


def solution(mesh):
    placed = (
        P(("parts", "gx"), None),
        P(None, ("parts", "gx")),
        P(("parts", "gx")),
        P(("parts", "gx")),
        P(("parts", "gx")),
        P(),
        P(),
        P(),
        P(),
        P(("parts", "gx"), None),
    )
    return jax.shard_map(
        on_device,
        mesh=mesh,
        in_specs=placed,
        out_specs=(
            P(("parts", "gx"), None),
            P(("parts", "gx"), None),
            P(("parts", "gx"), None),
            P(("parts", "gx"), None),
            P(("parts", "gx")),
        ),
        check_vma=False,
    )
```

time: 525 us -> 221 us (0.42)
  matrix products: 172 us -> 0 us
  waiting for transfers between devices: 167 us -> 32.5 us
  Pallas kernels: 0 us -> 130 us
  local copies, waits for them, and re-layouts: 104 us -> 13.3 us
  between operations: 14.5 us -> 0.72 us
  other arithmetic: 11.3 us -> 2.56 us
  starting transfers between devices: 29.3 us -> 21.3 us
    reduce_scatter x3 -> x0, waiting for transfers between devices: 158 us -> none  [the longest x1 96.2 us: on_device(): lax.psum_scatter(lax.dot_general(gathered, grad_hidden, (((0,), (0,)), ((...]
    dot_general x28 -> x0, matrix products: 132 us -> none  [the longest x4 32.9 us: attend_backward(): jnp.einsum('hqk,khd->qhd', grad_scores, keys, preferred_element_type=jnp....]
    pallas_call x0 -> x5, Pallas kernels: none -> 130 us  [the longest x1 56.9 us: on_device(): pl.pallas_call(functools.partial(reduce_kernel, count), out_shape=(shape(...]
    gather x8 -> x0, local copies, waits for them, and re-layouts: 54.3 us -> none  [the longest x1 34.9 us: on_device(): gathered = table[neighbours.T].reshape(tile_rows, -1)]
    sub x8 -> x0, matrix products: 39.9 us -> none  [softmax_weights(): raised = jnp.exp(scores - highest)]
    unnamed x1 -> x0, blocking collectives: 22.1 us -> none
    all_to_all x0 -> x1, blocking collectives: none -> 18.8 us  [swap(): lax.all_to_all(values.reshape(count, capacity, -1), 'gx', split_axis=0, c...]
    all_to_all x4 -> x3, waiting for transfers between devices: 8.65 us -> 25.3 us  [swap(): lax.all_to_all(values.reshape(count, capacity, -1), 'gx', split_axis=0, c...]
  transfers between devices with their start and end apart: 9 -> 5, of which waited for: 5 -> 4; matrix products, arithmetic and copies ran while one was open for 29% -> 2% of each run, Pallas kernels for 0% -> 11%
where the time goes in v1:
time: 221 us; the launch traced here: 219 us
  Pallas kernels  130 us (59%)
  waiting for transfers between devices  32.5 us (15%)
  starting transfers between devices  21.3 us (10%)
  blocking collectives  18.8 us (9%)
  local copies, waits for them, and re-layouts  13.3 us (6%)
  other arithmetic  2.56 us (1%)
    pallas_call x1, Pallas kernels, on_device(): pl.pallas_call(functools.partial(reduce_kernel, count), out_shape=(shape(...  56.9 us
    all_to_all x3, waiting for transfers between devices, swap(): lax.all_to_all(values.reshape(count, capacity, -1), 'gx', split_axis=0, c...  25.3 us
    pallas_call x1, Pallas kernels, on_device(): pl.pallas_call(conv_kernel, grid=(kernel,), out_shape=(shape((kernel, cha...  24.9 us
    pallas_call x1, Pallas kernels, on_device(): pl.pallas_call(attention_kernel, out_shape=(shape((slots, channels), BF16...  24.8 us
    pallas_call x1, Pallas kernels, on_device(): pl.pallas_call(backward_kernel, grid=(kernel,), out_shape=(shape((rows, c...  20.5 us
    all_to_all x1, blocking collectives, swap(): lax.all_to_all(values.reshape(count, capacity, -1), 'gx', split_axis=0, c...  18.8 us
    all_to_all x3, starting transfers between devices, swap(): lax.all_to_all(values.reshape(count, capacity, -1), 'gx', split_axis=0, c...  16 us
    ppermute x1, waiting for transfers between devices, on_device(): low = lax.ppermute(rim_feats[rim:], 'gx', forward)  5.55 us
  transfers between devices with their start and end apart: 5, of which 4 were waited for; matrix products, arithmetic and copies ran while one was open for 2% of the time, Pallas kernels for 11%

profile of v1, /device:TPU:13, one launch (start us, length us, event | category | flops | bytes accessed | tf_op | source)
XLA Modules:
  0.0 218.8 jit_solution(1592658480132028831)
XLA Ops:
  0.6 1.4 copy.16.rim_col
  2.1 2.4 %start.1 = (bf16[128,256]{1,0:T(8,128)(2,1)}, bf16[1024,256]{1,0:T(8,128)(2,1)}) custom-call(bf16[512,256]{1,0:T(8,128)(2,1)} %feats.3, bf16[512,256]{1,0:T(8,128)(2,1)} %out_grad.1, s32[128,1]{1,0:T(8,128)} %copy.16.rim_col, s32[1,512]{1,0:T(1,128)} %bitcast.28), custom_call_target="tpu_custom_call" | custom-call | tf_op jit(solution)/shard_map/start/pallas_call | solution.py:257
  4.4 6.6 %all-to-all-start.1 = ((bf16[16,64,256]{2,1,0:T(8,128)(2,1)}), bf16[16,64,256]{2,1,0:T(8,128)(2,1)S(1)}, u32[]{:S(2)}, u32[]{:S(2)}) async-start(bf16[16,64,256]{2,1,0:T(8,128)(2,1)} %bitcast.23), calls=%async_computation.1 | async-start | bytes 1048576 | tf_op jit(solution)/shard_map/all_to_all | solution.py:271
  11.0 0.8 fusion
  11.8 3.3 %collective-permute-start = (bf16[64,256]{1,0:T(8,128)(2,1)S(1)}, bf16[64,256]{1,0:T(8,128)(2,1)S(1)}, u32[]{:S(2)}, u32[]{:S(2)}) collective-permute-start(bf16[64,256]{1,0:T(8,128)(2,1)S(1)} %get-tuple-element.34), channel_id=1, source_target_pairs={{0,1},{1,2},{2,3},{3,4},{4,5},{5,6},{6,7},{7,8},{8,9},{9,10},{10,1... | collective-permute-start | bytes 98312 | tf_op jit(solution)/shard_map/ppermute | solution.py:267
  15.1 1.9 collective-permute-start.1
  17.1 0.7 reshape.72.nbrs
  17.7 5.6 %collective-permute-done.low = bf16[64,256]{1,0:T(8,128)(2,1)S(1)} collective-permute-done((bf16[64,256]{1,0:T(8,128)(2,1)S(1)}, bf16[64,256]{1,0:T(8,128)(2,1)S(1)}, u32[]{:S(2)}, u32[]{:S(2)}) %collective-permute-start) | collective-permute-done | bytes 32800 | tf_op jit(solution)/shard_map/ppermute | solution.py:267
  23.3 1.7 collective-permute-done.1.high
  24.9 0.6 copy-done.7
  25.6 24.9 %conv.1 = (bf16[27,256,512]{2,1,0:T(8,128)(2,1)}, f32[512,256]{1,0:T(8,128)}, bf16[1024,256]{1,0:T(8,128)(2,1)}) custom-call(bf16[512,256]{1,0:T(8,128)(2,1)} %feats.3, bf16[64,256]{1,0:T(8,128)(2,1)} %copy-done.6, bf16[64,256]{1,0:T(8,128)(2,1)} %copy-done.7, s32[27,1,512]{2,1,0:T(1,128)} %reshape.72.nbrs, bf16[6912,256]{1,0:T(8,128)(2,1)} %weight.1, ...), custom_call_target="tpu_custom_call" | custom-call | tf_op jit(solution)/shard_map/conv/pallas_call | solution.py:280
  50.5 4.5 %all-to-all-start = ((bf16[16,64,256]{2,1,0:T(8,128)(2,1)}), bf16[16,64,256]{2,1,0:T(8,128)(2,1)S(1)}, u32[]{:S(2)}, u32[]{:S(2)}) async-start(bf16[16,64,256]{2,1,0:T(8,128)(2,1)} %bitcast.24), calls=%async_computation | async-start | bytes 1048576 | tf_op jit(solution)/shard_map/all_to_all | solution.py:271
  55.0 0.9 copy.17.rows_col
  55.9 12.7 %all-to-all-done = bf16[16,64,256]{2,1,0:T(8,128)(2,1)S(1)} async-done(((bf16[16,64,256]{2,1,0:T(8,128)(2,1)}), bf16[16,64,256]{2,1,0:T(8,128)(2,1)S(1)}, u32[]{:S(2)}, u32[]{:S(2)}) %all-to-all-start) | async-done | bytes 524320 | tf_op jit(solution)/shard_map/all_to_all | solution.py:271
  68.6 0.8 copy-done.2
  69.4 24.8 %attention.1 = (bf16[1024,256]{1,0:T(8,128)(2,1)}, bf16[1024,256]{1,0:T(8,128)(2,1)}, f32[256,768]{1,0:T(8,128)}, f32[256,256]{1,0:T(8,128)}) custom-call(bf16[1024,256]{1,0:T(8,128)(2,1)} %bitcast.22, bf16[1024,256]{1,0:T(8,128)(2,1)} %bitcast.21, s32[1,512]{1,0:T(1,128)} %bitcast.31, s32[512,1]{1,0:T(8,128)} %copy.17.rows_col, bf16[256,768]{1,0:T(8,128)(2,1)} %qkv_w.1, ...), custom_call_target="tpu_custom_call" | custom-call | tf_op jit(solution)/shard_map/attention/pallas_call | solution.py:311
  94.2 18.8 %all_to_all.20 = bf16[16,64,256]{2,1,0:T(8,128)(2,1)} all-to-all(bf16[16,64,256]{2,1,0:T(8,128)(2,1)} %bitcast.26), channel_id=1, replica_groups=mesh['parts'=2,'gx'=16] {'gx'}, dimensions={0} | all-to-all | bytes 1048576 | tf_op jit(solution)/shard_map/all_to_all | solution.py:271
  113.0 5.0 %all-to-all-start.3 = ((bf16[16,64,256]{2,1,0:T(8,128)(2,1)}), bf16[16,64,256]{2,1,0:T(8,128)(2,1)S(1)}, u32[]{:S(2)}, u32[]{:S(2)}) async-start(bf16[16,64,256]{2,1,0:T(8,128)(2,1)} %bitcast.25), calls=%async_computation.3 | async-start | bytes 1048576 | tf_op jit(solution)/shard_map/all_to_all | solution.py:271
  118.0 0.8 copy.18.slot_col
  118.8 0.2 reshape.86
  119.0 12.6 %all-to-all-done.3 = bf16[16,64,256]{2,1,0:T(8,128)(2,1)S(1)} async-done(((bf16[16,64,256]{2,1,0:T(8,128)(2,1)}), bf16[16,64,256]{2,1,0:T(8,128)(2,1)S(1)}, u32[]{:S(2)}, u32[]{:S(2)}) %all-to-all-start.3) | async-done | bytes 524320 | tf_op jit(solution)/shard_map/all_to_all | solution.py:271
  131.6 0.8 copy-done
  132.4 20.5 %backward.1 = (bf16[512,256]{1,0:T(8,128)(2,1)}, f32[1,256]{1,0:T(1,128)}, f32[6912,256]{1,0:T(8,128)}) custom-call(f32[512,256]{1,0:T(8,128)} %get-tuple-element.20.hidden, bf16[1024,256]{1,0:T(8,128)(2,1)} %bitcast.19, bf16[1024,256]{1,0:T(8,128)(2,1)} %bitcast.20, bf16[512,256]{1,0:T(8,128)(2,1)} %out_grad.1, f32[1,256]{1,0:T(1,128)} %bitcast.34, ...), custom_call_target="tpu_custom_call" | custom-call | tf_op jit(solution)/shard_map/backward/pallas_call | solution.py:335
  152.9 0.5 broadcast.9
  153.4 1.3 reduce.4
  154.9 1.2 select_maximum_fusion.small
  156.1 56.9 %reduce.5 = (f32[432,256]{1,0:T(8,128)}, f32[80,256]{1,0:T(8,128)}) custom-call(f32[16,432,256]{2,1,0:T(8,128)} %bitcast.18, f32[16,80,256]{2,1,0:T(8,128)} %select_maximum_fusion.small), custom_call_target="tpu_custom_call" | custom-call | tf_op jit(solution)/shard_map/reduce/pallas_call | solution.py:383
  213.0 0.8 slice.17
  213.8 1.3 slice.18
  215.2 1.2 slice_bitcast_fusion
  216.3 0.6 reshape.89
  217.0 1.8 copy.20
  (19 shorter events, 0.1 us)
Async XLA Ops:
  0.6 16.4 %copy-start.5 = (s32[27,512]{1,0:T(8,128)S(1)}, s32[27,512]{1,0:T(8,128)}, u32[]{:S(2)}) copy-start(s32[27,512]{1,0:T(8,128)} %param.11) | copy-start | bytes 165892
  4.4 46.0 %all-to-all-start.1 = ((bf16[16,64,256]{2,1,0:T(8,128)(2,1)}), bf16[16,64,256]{2,1,0:T(8,128)(2,1)S(1)}, u32[]{:S(2)}, u32[]{:S(2)}) async-start(bf16[16,64,256]{2,1,0:T(8,128)(2,1)} %bitcast.23), calls=%async_computation.1 | async-start | bytes 1048576 | tf_op jit(solution)/shard_map/all_to_all | solution.py:271
  11.8 11.5 %collective-permute-start = (bf16[64,256]{1,0:T(8,128)(2,1)S(1)}, bf16[64,256]{1,0:T(8,128)(2,1)S(1)}, u32[]{:S(2)}, u32[]{:S(2)}) collective-permute-start(bf16[64,256]{1,0:T(8,128)(2,1)S(1)} %get-tuple-element.34), channel_id=1, source_target_pairs={{0,1},{1,2},{2,3},{3,4},{4,5},{5,6},{6,7},{7,8},{8,9},{9,10},{10,1... | collective-permute-start | bytes 98312 | tf_op jit(solution)/shard_map/ppermute | solution.py:267
  15.1 9.8 %collective-permute-start.1 = (bf16[64,256]{1,0:T(8,128)(2,1)S(1)}, bf16[64,256]{1,0:T(8,128)(2,1)S(1)}, u32[]{:S(2)}, u32[]{:S(2)}) collective-permute-start(bf16[64,256]{1,0:T(8,128)(2,1)S(1)} %get-tuple-element.33), channel_id=1, source_target_pairs={{1,0},{2,1},{3,2},{4,3},{5,4},{6,5},{7,6},{8,7},{9,8},{10,9},{11,1... | collective-permute-start | bytes 98312 | tf_op jit(solution)/shard_map/ppermute | solution.py:268
  23.3 1.7 copy-start.6
  24.9 0.6 copy-start.7
  25.6 29.4 %copy-start.9 = (s32[512]{0:T(512)S(1)}, s32[512]{0:T(512)}, u32[]{:S(2)}) copy-start(s32[512]{0:T(512)} %param.14) | copy-start | bytes 6148
  50.5 18.1 %copy-start.1 = (bf16[16,64,256]{2,1,0:T(8,128)(2,1)}, bf16[16,64,256]{2,1,0:T(8,128)(2,1)S(1)}, u32[]{:S(2)}) copy-start(bf16[16,64,256]{2,1,0:T(8,128)(2,1)S(1)} %all-to-all-done.1) | copy-start | bytes 1572868
  50.5 18.1 %all-to-all-start = ((bf16[16,64,256]{2,1,0:T(8,128)(2,1)}), bf16[16,64,256]{2,1,0:T(8,128)(2,1)S(1)}, u32[]{:S(2)}, u32[]{:S(2)}) async-start(bf16[16,64,256]{2,1,0:T(8,128)(2,1)} %bitcast.24), calls=%async_computation | async-start | bytes 1048576 | tf_op jit(solution)/shard_map/all_to_all | solution.py:271
  68.6 0.8 copy-start.2
  94.2 23.8 %copy-start.8 = (s32[512]{0:T(512)S(1)}, s32[512]{0:T(512)}, u32[]{:S(2)}) copy-start(s32[512]{0:T(512)} %param.13) | copy-start | bytes 6148
  94.2 24.7 %copy-start.3 = (f32[256,768]{1,0:T(8,128)S(1)}, f32[256,768]{1,0:T(8,128)}, u32[]{:S(2)}) copy-start(f32[256,768]{1,0:T(8,128)} %get-tuple-element.28) | copy-start | bytes 2359300
  113.0 18.6 %all-to-all-start.3 = ((bf16[16,64,256]{2,1,0:T(8,128)(2,1)}), bf16[16,64,256]{2,1,0:T(8,128)(2,1)S(1)}, u32[]{:S(2)}, u32[]{:S(2)}) async-start(bf16[16,64,256]{2,1,0:T(8,128)(2,1)} %bitcast.25), calls=%async_computation.3 | async-start | bytes 1048576 | tf_op jit(solution)/shard_map/all_to_all | solution.py:271
  131.6 0.8 copy-start
  132.4 22.5 %copy-start.4 = (f32[256,256]{1,0:T(8,128)S(1)}, f32[256,256]{1,0:T(8,128)}, u32[]{:S(2)}) copy-start(f32[256,256]{1,0:T(8,128)} %get-tuple-element.29) | copy-start | bytes 786436

commit v2 on v1

v2 whole, which is shorter than its diff:
```python
import functools

import jax
import jax.numpy as jnp
from jax import lax
from jax.experimental import pallas as pl
from jax.experimental.pallas import tpu as pltpu
from jax.sharding import PartitionSpec as P

HEADS = 16
HEAD = 16
LIMIT = 56 * 1024 * 1024
F32 = jnp.float32
BF16 = jnp.bfloat16
VMEM = pl.BlockSpec(memory_space=pltpu.VMEM)


def dot(a, b, ca=1, cb=0):
    return lax.dot_general(a, b, (((ca,), (cb,)), ((), ())), preferred_element_type=F32)


def hot_rows(index_row, count):
    rows = lax.broadcasted_iota(jnp.int32, (count, index_row.shape[1]), 0)
    return jnp.where(rows == index_row, 1.0, 0.0).astype(BF16)


def hot_columns(index_column, count):
    columns = lax.broadcasted_iota(jnp.int32, (index_column.shape[0], count), 1)
    return jnp.where(columns == index_column, 1.0, 0.0).astype(BF16)


def normalise(hidden):
    centred = hidden - jnp.mean(hidden, axis=-1, keepdims=True)
    inv_std = 1.0 / jnp.sqrt(jnp.mean(centred * centred, axis=-1, keepdims=True) + 1e-05)
    return centred * inv_std, inv_std


def copy_to(source, target, send, recv, device):
    return pltpu.make_async_remote_copy(
        src_ref=source,
        dst_ref=target,
        send_sem=send,
        recv_sem=recv,
        device_id={"gx": device},
        device_id_type=pl.DeviceIdType.MESH,
    )


def greet(devices):
    barrier = pltpu.get_barrier_semaphore()
    for device in devices:
        pl.semaphore_signal(
            barrier, inc=1, device_id={"gx": device}, device_id_type=pl.DeviceIdType.MESH
        )
    pl.semaphore_wait(barrier, len(devices))


class Exchange:
    def __init__(self, count, me, source, target, send, recv):
        self.own = pltpu.make_async_copy(source.at[me], target.at[me], send.at[0])
        self.sends = []
        self.recvs = []
        for step in range(1, count):
            peer = lax.rem(me + step, count)
            sender = lax.rem(me + count - step, count)
            self.sends.append(
                copy_to(source.at[peer], target.at[me], send.at[step], recv.at[step], peer)
            )
            self.recvs.append(
                copy_to(source.at[peer], target.at[sender], send.at[step], recv.at[step], peer)
            )

    def start(self):
        for one in self.sends:
            one.start()
        self.own.start()

    def arrive(self):
        self.own.wait()
        for one in self.recvs:
            one.wait_recv()

    def leave(self):
        for one in self.sends:
            one.wait_send()


def put_slots(target, values):
    for block in range(target.shape[0]):
        cap = target.shape[1]
        target[block] = values[block * cap : (block + 1) * cap]


def conv_kernel(
    count, feats, grads, rim_col, nbrs, weight, gain, slot_row,
    gathered_out, hidden_out, recv_normed, recv_grad,
    table, acc, rim_send, rim_recv, grad_slots, normed_slots,
    rim_out, rim_in, grad_out, grad_in, normed_out, normed_in,
):
    k = pl.program_id(0)
    rows, channels = feats.shape
    rim = rim_recv.shape[1]
    slots = count * grad_slots.shape[1]
    me = lax.axis_index("gx")
    before, after = lax.rem(me + count - 1, count), lax.rem(me + 1, count)
    to_before = copy_to(rim_send.at[0], rim_recv.at[1], rim_out.at[0], rim_in.at[1], before)
    to_after = copy_to(rim_send.at[1], rim_recv.at[0], rim_out.at[1], rim_in.at[0], after)
    grad_swap = Exchange(count, me, grad_slots, recv_grad, grad_out, grad_in)
    normed_swap = Exchange(count, me, normed_slots, recv_normed, normed_out, normed_in)

    @pl.when(k == 0)
    def _():
        picked = dot(hot_columns(rim_col[...], rows), feats[...]).astype(BF16)
        rim_send[0] = picked[:rim]
        rim_send[1] = picked[rim:]
        greet([lax.rem(me + step, count) for step in range(1, count)])
        to_before.start()
        to_after.start()
        put_slots(grad_slots, dot(hot_rows(slot_row[...], slots), grads[...]).astype(BF16))
        grad_swap.start()
        table[:, :rows] = feats[...].T
        acc[...] = jnp.zeros_like(acc)
        to_before.wait_recv()
        to_after.wait_recv()
        low = jnp.where(me > 0, 1.0, 0.0) * rim_recv[0].astype(F32)
        high = jnp.where(me < count - 1, 1.0, 0.0) * rim_recv[1].astype(F32)
        table[:, rows : rows + rim] = low.T.astype(BF16)
        table[:, rows + rim :] = high.T.astype(BF16)
        to_before.wait_send()
        to_after.wait_send()

    total = acc[...]
    for one in range(nbrs.shape[0]):
        gathered = dot(table[...], hot_rows(nbrs[one], rows + 2 * rim)).astype(BF16)
        gathered_out[one] = gathered
        total += dot(weight[one], gathered, 0, 0)
    acc[...] = total

    @pl.when(k == pl.num_programs(0) - 1)
    def _():
        hidden = feats[...].astype(F32) + acc[...].T
        hidden_out[...] = hidden
        standard, _ = normalise(hidden)
        normed = (standard * gain[...]).astype(BF16)
        put_slots(normed_slots, dot(hot_rows(slot_row[...], slots), normed).astype(BF16))
        normed_swap.start()
        grad_swap.arrive()
        grad_swap.leave()
        normed_swap.arrive()
        normed_swap.leave()


def attention_kernel(
    count, recv_normed, recv_grad, rows_row, rows_col, qkv_w, proj_w,
    out_proj, back_grad, qkv_term, proj_term,
    qkv_t, scaled_t, up_t, att_t, grad_t, grad_slots, sent, received,
):
    me = lax.axis_index("gx")
    swap = Exchange(count, me, grad_slots, back_grad, sent, received)
    channels = proj_w.shape[0]
    slots = recv_normed.shape[0]
    picks = hot_columns(rows_col[...], slots)
    patch_in = dot(picks, recv_normed[...]).astype(BF16)
    patch_grad = dot(picks, recv_grad[...]).astype(BF16)
    qkv = dot(patch_in, qkv_w[...]).T
    qkv_t[...] = qkv.astype(BF16)
    scaled_t[...] = (qkv_t[:channels, :].astype(F32) * 0.25).astype(BF16)
    up_t[...] = dot(patch_grad, proj_w[...], 1, 1).T.astype(BF16)

    def head(h, carry):
        def part(ref, base=0):
            return ref[pl.ds(pl.multiple_of(base + h * HEAD, HEAD), HEAD), :]

        query, keys, values = part(qkv_t), part(qkv_t, channels), part(qkv_t, 2 * channels)
        query_low = part(scaled_t)
        up = part(up_t)
        up_low = (up.astype(F32) * 0.25).astype(BF16)
        scores = dot(keys, query_low, 0, 0)
        raised = jnp.exp(scores - jnp.max(scores, axis=0, keepdims=True))
        probs = raised * (1.0 / jnp.sum(raised, axis=0, keepdims=True))
        probs_low = probs.astype(BF16)
        grad_probs = dot(values, up_low, 0, 0)
        total = jnp.sum(grad_probs * probs, axis=0, keepdims=True)
        grad_scores = (probs * (grad_probs - total)).astype(BF16)

        def put(ref, value, base=0):
            ref[pl.ds(pl.multiple_of(base + h * HEAD, HEAD), HEAD), :] = value.astype(BF16)

        put(att_t, dot(values, probs_low))
        put(grad_t, dot(up, probs_low, 1, 1), 2 * channels)
        put(grad_t, dot(keys, grad_scores))
        put(grad_t, dot(query, grad_scores, 1, 1), channels)
        return carry

    lax.fori_loop(0, HEADS, head, 0, unroll=2)
    back = hot_rows(rows_row[...], slots)
    grad_qkv = grad_t[...].astype(F32).T.astype(BF16)
    grad_normed = dot(grad_qkv, qkv_w[...], 1, 1).astype(BF16)
    put_slots(grad_slots, dot(back, grad_normed).astype(BF16))
    greet([lax.rem(me + step, count) for step in range(1, count)])
    swap.start()
    proj_out = dot(att_t[...], proj_w[...], 0, 0).astype(BF16)
    out_proj[...] = dot(back, proj_out).astype(BF16)
    proj_term[...] = dot(att_t[...], patch_grad)
    qkv_term[...] = dot(patch_in, grad_qkv, 0, 0)
    swap.arrive()
    swap.leave()


def backward_kernel(
    count, gain_row, hidden, proj_slots, back_grad, out_grad, gain, slot_col, small, gathered,
    block_out, total_out,
    grad_hidden, columns, proj_back, near_send, near_recv, mid_send, mid_recv, far_send, far_recv,
    load, proj_sent, proj_got, near_sent, near_got, mid_sent, mid_got, far_sent, far_got,
):
    me = lax.axis_index("gx")
    core = lax.rem(me, 2)
    chip = me // 2
    side = lax.rem(chip, 2)
    group = chip // 2
    groups = count // 4
    conv_rows = columns.shape[1]
    order = [lax.rem(group + step, groups) for step in range(1, groups + 1)]

    def device(of_group, of_side, of_core):
        return of_group * 4 + of_side * 2 + of_core

    loading = pltpu.make_async_copy(gathered, columns, load.at[0])
    loading.start()
    greet([lax.rem(me + step, count) for step in range(1, count)])
    proj_swap = Exchange(count, me, proj_slots, proj_back, proj_sent, proj_got)
    proj_swap.start()

    picks = hot_columns(slot_col[...], back_grad.shape[0])
    grad_back = dot(picks, back_grad[...])
    standard, inv_std = normalise(hidden[...])
    gain_term = jnp.sum(grad_back * standard, axis=0, keepdims=True)
    scaled = grad_back * gain[...]
    grad_hidden[...] = (
        out_grad[...].astype(F32)
        + inv_std
        * (
            scaled
            - jnp.mean(scaled, axis=-1, keepdims=True)
            - standard * jnp.mean(scaled * standard, axis=-1, keepdims=True)
        )
    ).astype(BF16)
    small_rows, channels = small.shape[1:]
    at_row = lax.broadcasted_iota(jnp.int32, (small_rows, channels), 0)
    gain_part = jnp.where(at_row == gain_row, 1.0, 0.0) * gain_term
    loading.wait()

    near = []
    for step, other in enumerate(order):
        for part, of_side in enumerate((1 - side, side)):
            place = 2 * step + part
            theirs = device(other, of_side, 1 - core)
            near_send[place, :conv_rows] = dot(columns[theirs], grad_hidden[...])
            near_send[place, conv_rows:] = small[theirs] + gain_part
            one = copy_to(near_send.at[place], near_recv.at[place], near_sent.at[place],
                          near_got.at[place], device(group, side, 1 - core))
            one.start()
            near.append(one)

    def both_cores(place, mine):
        conv = dot(columns[mine], grad_hidden[...])
        near[place].wait_recv()
        return (
            conv + near_recv[place, :conv_rows],
            small[mine] + gain_part + near_recv[place, conv_rows:],
        )

    mid = []
    for step, other in enumerate(order):
        conv, rest = both_cores(2 * step, device(other, 1 - side, core))
        mid_send[step, :conv_rows] = conv.astype(BF16)
        mid_send[step, conv_rows:] = rest.astype(BF16)
        one = copy_to(mid_send.at[step], mid_recv.at[step], mid_sent.at[step], mid_got.at[step],
                      device(group, 1 - side, core))
        one.start()
        mid.append(one)
    far = []
    for step, other in enumerate(order):
        conv, rest = both_cores(2 * step + 1, device(other, side, core))
        mid[step].wait_recv()
        conv += mid_recv[step, :conv_rows].astype(F32)
        rest += mid_recv[step, conv_rows:].astype(F32)
        if step < groups - 1:
            far_send[step, :conv_rows] = conv.astype(BF16)
            far_send[step, conv_rows:] = rest.astype(BF16)
            one = copy_to(far_send.at[step], far_recv.at[step], far_sent.at[step],
                          far_got.at[step], device(other, side, core))
            one.start()
            far.append(one)
        else:
            total_out[:conv_rows] = conv
            total_out[conv_rows:] = rest
    proj_swap.arrive()
    back_proj = dot(picks, proj_back[...].reshape(back_grad.shape))
    block_out[...] = (hidden[...] + back_proj).astype(BF16)
    for step in range(groups - 1):
        far[step].wait_recv()
        total_out[...] += far_recv[step].astype(F32)
    proj_swap.leave()
    for one in near + mid + far:
        one.wait_send()


def params(**more):
    return pltpu.CompilerParams(vmem_limit_bytes=LIMIT, **more)


def shape(dims, dtype):
    return jax.ShapeDtypeStruct(dims, dtype)


def on_device(
    features,
    neighbours,
    rim_rows,
    tile_slot,
    patch_rows,
    conv_weight,
    norm_gain,
    qkv_weight,
    proj_weight,
    out_grad,
):
    rows, channels = features.shape
    count = lax.axis_size("gx")
    capacity = 2 * rows // count
    slots = count * capacity
    rim = rim_rows.shape[0] // 2
    kernel = neighbours.shape[0]
    gain = norm_gain.reshape(1, channels)
    slot_row, slot_col = tile_slot.reshape(1, rows), tile_slot.reshape(rows, 1)
    rows_row, rows_col = patch_rows.reshape(1, rows), patch_rows.reshape(rows, 1)

    def full(*dims):
        return pl.BlockSpec(dims, lambda k: (0,) * len(dims))

    def dma(size):
        return pltpu.SemaphoreType.DMA((size,))

    anywhere = pl.BlockSpec(memory_space=pl.ANY)
    blocks = (count, capacity, channels)
    each = 9 if kernel % 9 == 0 else 1
    gathered, hidden, recv_normed, recv_grad = pl.pallas_call(
        functools.partial(conv_kernel, count),
        grid=(kernel // each,),
        out_shape=(
            shape((kernel, channels, rows), BF16),
            shape((rows, channels), F32),
            shape(blocks, BF16),
            shape(blocks, BF16),
        ),
        in_specs=[
            full(rows, channels),
            full(rows, channels),
            full(2 * rim, 1),
            pl.BlockSpec((each, 1, rows), lambda k: (k, 0, 0)),
            pl.BlockSpec((each, channels, channels), lambda k: (k, 0, 0)),
            full(1, channels),
            full(1, rows),
        ],
        out_specs=(
            pl.BlockSpec((each, channels, rows), lambda k: (k, 0, 0)),
            full(rows, channels),
            anywhere,
            anywhere,
        ),
        scratch_shapes=[
            pltpu.VMEM((channels, rows + 2 * rim), BF16),
            pltpu.VMEM((channels, rows), F32),
            pltpu.VMEM((2, rim, channels), BF16),
            pltpu.VMEM((2, rim, channels), BF16),
            pltpu.VMEM(blocks, BF16),
            pltpu.VMEM(blocks, BF16),
            dma(2), dma(2), dma(count), dma(count), dma(count), dma(count),
        ],
        compiler_params=params(collective_id=1, has_side_effects=True),
        name="conv",
    )(
        features, out_grad, rim_rows.reshape(2 * rim, 1), neighbours.reshape(kernel, 1, rows),
        conv_weight.reshape(kernel, channels, channels), gain, slot_row,
    )

    proj_slots, back_grad, qkv_term, proj_term = pl.pallas_call(
        functools.partial(attention_kernel, count),
        out_shape=(
            shape((slots, channels), BF16),
            shape(blocks, BF16),
            shape((channels, 3 * channels), F32),
            shape((channels, channels), F32),
        ),
        in_specs=[VMEM] * 6,
        out_specs=(VMEM, anywhere, VMEM, VMEM),
        scratch_shapes=[
            pltpu.VMEM((3 * channels, rows), BF16),
            pltpu.VMEM((channels, rows), BF16),
            pltpu.VMEM((channels, rows), BF16),
            pltpu.VMEM((channels, rows), BF16),
            pltpu.VMEM((3 * channels, rows), BF16),
            pltpu.VMEM(blocks, BF16),
            dma(count), dma(count),
        ],
        compiler_params=params(collective_id=2, has_side_effects=True),
        name="attention",
    )(
        recv_normed.reshape(slots, channels), recv_grad.reshape(slots, channels),
        rows_row, rows_col, qkv_weight, proj_weight,
    )

    conv_rows = kernel * channels // count
    padded_rows = -(-conv_rows // 16) * 16
    one = channels // count
    gain_row = 4 * one
    small_rows = -(-(gain_row + 1) // 16) * 16
    small = jnp.concatenate(
        [
            qkv_term.reshape(count, 3 * one, channels),
            proj_term.reshape(count, one, channels),
            jnp.zeros((count, small_rows - gain_row, channels), F32),
        ],
        axis=1,
    )
    columns = gathered.reshape(count, conv_rows, rows)
    if padded_rows > conv_rows:
        columns = jnp.pad(columns, ((0, 0), (0, padded_rows - conv_rows), (0, 0)))
    chips, groups, chunk = count // 2, count // 4, padded_rows + small_rows
    block_out, total = pl.pallas_call(
        functools.partial(backward_kernel, count, gain_row),
        out_shape=(shape((rows, channels), BF16), shape((chunk, channels), F32)),
        in_specs=[VMEM] * 7 + [anywhere],
        out_specs=(VMEM, VMEM),
        scratch_shapes=[
            pltpu.VMEM((rows, channels), BF16),
            pltpu.VMEM((count, padded_rows, rows), BF16),
            pltpu.VMEM(blocks, BF16),
            pltpu.VMEM((chips, chunk, channels), F32),
            pltpu.VMEM((chips, chunk, channels), F32),
            pltpu.VMEM((groups, chunk, channels), BF16),
            pltpu.VMEM((groups, chunk, channels), BF16),
            pltpu.VMEM((groups - 1, chunk, channels), BF16),
            pltpu.VMEM((groups - 1, chunk, channels), BF16),
            dma(1), dma(count), dma(count), dma(chips), dma(chips),
            dma(groups), dma(groups), dma(groups), dma(groups),
        ],
        compiler_params=params(collective_id=3, has_side_effects=True),
        name="backward",
    )(
        hidden, proj_slots.reshape(blocks), back_grad.reshape(slots, channels), out_grad, gain,
        slot_col, small, columns,
    )
    small_sum = total[padded_rows:]
    return (
        block_out,
        total[:conv_rows],
        small_sum[: 3 * one].reshape(one, 3 * channels),
        small_sum[3 * one : gain_row],
        lax.dynamic_slice_in_dim(small_sum[gain_row], lax.axis_index("gx") * one, one),
    )


def solution(mesh):
    placed = (
        P(("parts", "gx"), None),
        P(None, ("parts", "gx")),
        P(("parts", "gx")),
        P(("parts", "gx")),
        P(("parts", "gx")),
        P(),
        P(),
        P(),
        P(),
        P(("parts", "gx"), None),
    )
    return jax.shard_map(
        on_device,
        mesh=mesh,
        in_specs=placed,
        out_specs=(
            P(("parts", "gx"), None),
            P(("parts", "gx"), None),
            P(("parts", "gx"), None),
            P(("parts", "gx"), None),
            P(("parts", "gx")),
        ),
        check_vma=False,
    )
```

time: 221 us -> 138 us (0.62)
  waiting for transfers between devices: 32.5 us -> 0 us
  starting transfers between devices: 21.3 us -> 0 us
  blocking collectives: 18.8 us -> 0 us
  Pallas kernels: 130 us -> 122 us
    all_to_all x3 -> x0, waiting for transfers between devices: 25.3 us -> none  [swap(): lax.all_to_all(values.reshape(count, capacity, -1), 'gx', split_axis=0, c...]
    all_to_all x1 -> x0, blocking collectives: 18.8 us -> none  [swap(): lax.all_to_all(values.reshape(count, capacity, -1), 'gx', split_axis=0, c...]
    all_to_all x3 -> x0, starting transfers between devices: 16 us -> none  [swap(): lax.all_to_all(values.reshape(count, capacity, -1), 'gx', split_axis=0, c...]
    pallas_call x5 -> x3, Pallas kernels: 130 us -> 122 us  [the longest x1 44.5 us: on_device(): pl.pallas_call(functools.partial(backward_kernel, count, gain_row), out_s...]
    ppermute x2 -> x0, waiting for transfers between devices: 7.23 us -> none  [the longest x1 5.55 us: on_device(): low = lax.ppermute(rim_feats[rim:], 'gx', forward)]
    ppermute x2 -> x0, starting transfers between devices: 5.25 us -> none  [the longest x1 3.33 us: on_device(): low = lax.ppermute(rim_feats[rim:], 'gx', forward)]
    unnamed x21 -> x9, local copies, waits for them, and re-layouts: 4.03 us -> 0.72 us
  transfers between devices with their start and end apart: 5 -> 0, of which waited for: 4 -> 0; matrix products, arithmetic and copies ran while one was open for 2% -> 0% of each run, Pallas kernels for 11% -> 0%
where the time goes in v2:
time: 138 us; the launch traced here: 137 us
  Pallas kernels  122 us (88%)
  local copies, waits for them, and re-layouts  12.6 us (9%)
    pallas_call x1, Pallas kernels, on_device(): pl.pallas_call(functools.partial(backward_kernel, count, gain_row), out_s...  44.5 us
    pallas_call x1, Pallas kernels, on_device(): pl.pallas_call(functools.partial(attention_kernel, count), out_shape=(sha...  41.1 us
    pallas_call x1, Pallas kernels, on_device(): pl.pallas_call(functools.partial(conv_kernel, count), grid=(kernel // eac...  36.6 us

profile of v2, /device:TPU:13, one launch (start us, length us, event | category | flops | bytes accessed | tf_op | source)
XLA Modules:
  0.0 136.9 jit_solution(9823777660765249893)
XLA Ops:
  0.6 1.4 %copy.16.rim_col = s32[128,1]{1,0:T(8,128)} copy(s32[128,1]{0,1:T(1,128)} %bitcast.28) | data formatting | bytes 1024 | tf_op jit(solution)/shard_map/reshape | solution.py:384
  2.0 1.5 %reshape.60.nbrs = s32[27,1,512]{2,1,0:T(1,128)} reshape(s32[27,512]{1,0:T(8,128)} %param.11) | data formatting | bytes 110592 | tf_op jit(solution)/shard_map/reshape | solution.py:384
  3.5 0.0 copy-start.3
  3.5 36.6 %conv.1 = (bf16[27,256,512]{2,1,0:T(8,128)(2,1)}, f32[512,256]{1,0:T(8,128)}, bf16[16,64,256]{2,1,0:T(8,128)(2,1)}, bf16[16,64,256]{2,1,0:T(8,128)(2,1)}) custom-call(bf16[512,256]{1,0:T(8,128)(2,1)} %feats.1, bf16[512,256]{1,0:T(8,128)(2,1)} %out_grad.1, s32[128,1]{1,0:T(8,128)} %copy.16.rim_col, s32[27,1,512]{2,1,0:T(1,128)} %reshape.60.nbrs, ...), custom_call_target="tpu_custom_call" | custom-call | tf_op jit(solution)/shard_map/conv/pallas_call | solution.py:348
  40.2 0.0 copy-done.3
  40.2 0.9 copy.17.rows_col
  41.0 41.1 %attention.1 = (bf16[1024,256]{1,0:T(8,128)(2,1)}, bf16[16,64,256]{2,1,0:T(8,128)(2,1)}, f32[256,768]{1,0:T(8,128)}, f32[256,256]{1,0:T(8,128)}) custom-call(bf16[1024,256]{1,0:T(8,128)(2,1)} %bitcast.17, bf16[1024,256]{1,0:T(8,128)(2,1)} %bitcast.18, s32[1,512]{1,0:T(1,128)} %bitcast.24, s32[512,1]{1,0:T(8,128)} %copy.17.rows_col, bf16[256,768]{1,0:T(8,128)(2,1)} %qkv_w.1, ...), custom_call_target="tpu_custom_call" | custom-call | tf_op jit(solution)/shard_map/attention/pallas_call | solution.py:388
  82.2 0.0 copy-start
  82.2 1.3 reshape.71
  83.5 0.0 copy-start.2
  83.6 0.1 pad.2.clone
  83.6 0.0 copy-done
  83.6 1.3 maximum_maximum_fusion.small
  84.9 0.0 copy-done.2
  84.9 0.9 copy.18.slot_col
  85.8 44.5 %backward.1 = (bf16[512,256]{1,0:T(8,128)(2,1)}, f32[512,256]{1,0:T(8,128)}) custom-call(f32[512,256]{1,0:T(8,128)} %get-tuple-element.15.hidden, bf16[16,64,256]{2,1,0:T(8,128)(2,1)} %bitcast.19, bf16[1024,256]{1,0:T(8,128)(2,1)} %bitcast.20, bf16[512,256]{1,0:T(8,128)(2,1)} %out_grad.1, f32[1,256]{1,0:T(1,128)} %bitcast.27, s32[512,1]{1,0:T(8,128)} %copy.18.slot_col, ...), custom_call_target="tpu_custom_call" | custom-call | tf_op jit(solution)/shard_map/backward/pallas_call | solution.py:431
  130.3 0.0 copy-start.1
  130.3 0.7 slice.19
  131.0 0.6 dynamic-slice_bitcast_fusion
  131.6 1.8 %slice.16 = f32[432,256]{1,0:T(8,128)} slice(f32[512,256]{1,0:T(8,128)} %get-tuple-element.24), slice={[0:432], [0:256]} | slice | bytes 884736 | tf_op jit(solution)/shard_map/slice | solution.py:458
  133.4 0.8 slice.17
  134.2 0.6 reshape.74
  134.9 1.3 slice.18
  136.2 0.0 copy-done.1
  136.2 0.7 copy.20
  (1 shorter events, 0.0 us)
Async XLA Ops:
  3.5 36.6 %copy-start.3 = (s32[512]{0:T(512)S(1)}, s32[512]{0:T(512)}, u32[]{:S(2)}) copy-start(s32[512]{0:T(512)} %param.14) | copy-start | bytes 6148
  82.2 1.5 %copy-start = (f32[256,256]{1,0:T(8,128)S(1)}, f32[256,256]{1,0:T(8,128)}, u32[]{:S(2)}) copy-start(f32[256,256]{1,0:T(8,128)} %get-tuple-element.21) | copy-start | bytes 786436
  83.5 1.4 %copy-start.2 = (s32[512]{0:T(512)S(1)}, s32[512]{0:T(512)}, u32[]{:S(2)}) copy-start(s32[512]{0:T(512)} %param.13) | copy-start | bytes 6148
  130.3 5.9 %copy-start.1 = (bf16[512,256]{1,0:T(8,128)(2,1)S(1)}, bf16[512,256]{1,0:T(8,128)(2,1)}, u32[]{:S(2)}) copy-start(bf16[512,256]{1,0:T(8,128)(2,1)} %get-tuple-element.30) | copy-start | bytes 786436

commit v3 on v2

--- a/solution.py
+++ b/solution.py
@@ -24,7 +24,9 @@
     return jnp.where(rows == index_row, 1.0, 0.0).astype(BF16)
 
 
-def hot_columns(index_column, count):
+def hot_columns(index_row, count):
+    wide = jnp.broadcast_to(index_row.astype(F32), (8, index_row.shape[1]))
+    index_column = wide.T[:, :1].astype(jnp.int32)
     columns = lax.broadcasted_iota(jnp.int32, (index_column.shape[0], count), 1)
     return jnp.where(columns == index_column, 1.0, 0.0).astype(BF16)
 
@@ -60,7 +62,7 @@
         self.own = pltpu.make_async_copy(source.at[me], target.at[me], send.at[0])
         self.sends = []
         self.recvs = []
-        for step in range(1, count):
+        for step in sorted(range(1, count), key=lambda step: abs(2 * step - count)):
             peer = lax.rem(me + step, count)
             sender = lax.rem(me + count - step, count)
             self.sends.append(
@@ -92,7 +94,7 @@
 
 
 def conv_kernel(
-    count, feats, grads, rim_col, nbrs, weight, gain, slot_row,
+    count, feats, grads, rim_row, nbrs, weight, gain, slot_row,
     gathered_out, hidden_out, recv_normed, recv_grad,
     table, acc, rim_send, rim_recv, grad_slots, normed_slots,
     rim_out, rim_in, grad_out, grad_in, normed_out, normed_in,
@@ -100,6 +102,7 @@
     k = pl.program_id(0)
     rows, channels = feats.shape
     rim = rim_recv.shape[1]
+    each = weight.shape[0]
     slots = count * grad_slots.shape[1]
     me = lax.axis_index("gx")
     before, after = lax.rem(me + count - 1, count), lax.rem(me + 1, count)
@@ -110,7 +113,7 @@
 
     @pl.when(k == 0)
     def _():
-        picked = dot(hot_columns(rim_col[...], rows), feats[...]).astype(BF16)
+        picked = dot(hot_columns(rim_row[...], rows), feats[...]).astype(BF16)
         rim_send[0] = picked[:rim]
         rim_send[1] = picked[rim:]
         greet([lax.rem(me + step, count) for step in range(1, count)])
@@ -130,8 +133,8 @@
         to_after.wait_send()
 
     total = acc[...]
-    for one in range(nbrs.shape[0]):
-        gathered = dot(table[...], hot_rows(nbrs[one], rows + 2 * rim)).astype(BF16)
+    for one in range(each):
+        gathered = dot(table[...], hot_rows(nbrs[pl.ds(k * each + one, 1), :], rows + 2 * rim)).astype(BF16)
         gathered_out[one] = gathered
         total += dot(weight[one], gathered, 0, 0)
     acc[...] = total
@@ -151,7 +154,7 @@
 
 
 def attention_kernel(
-    count, recv_normed, recv_grad, rows_row, rows_col, qkv_w, proj_w,
+    count, recv_normed, recv_grad, rows_row, qkv_w, proj_w,
     out_proj, back_grad, qkv_term, proj_term,
     qkv_t, scaled_t, up_t, att_t, grad_t, grad_slots, sent, received,
 ):
@@ -159,7 +162,7 @@
     swap = Exchange(count, me, grad_slots, back_grad, sent, received)
     channels = proj_w.shape[0]
     slots = recv_normed.shape[0]
-    picks = hot_columns(rows_col[...], slots)
+    picks = hot_columns(rows_row[...], slots)
     patch_in = dot(picks, recv_normed[...]).astype(BF16)
     patch_grad = dot(picks, recv_grad[...]).astype(BF16)
     qkv = dot(patch_in, qkv_w[...]).T
@@ -192,7 +195,7 @@
         put(grad_t, dot(query, grad_scores, 1, 1), channels)
         return carry
 
-    lax.fori_loop(0, HEADS, head, 0, unroll=2)
+    lax.fori_loop(0, HEADS, head, 0, unroll=4)
     back = hot_rows(rows_row[...], slots)
     grad_qkv = grad_t[...].astype(F32).T.astype(BF16)
     grad_normed = dot(grad_qkv, qkv_w[...], 1, 1).astype(BF16)
@@ -208,9 +211,11 @@
 
 
 def backward_kernel(
-    count, gain_row, hidden, proj_slots, back_grad, out_grad, gain, slot_col, small, gathered,
-    block_out, total_out,
-    grad_hidden, columns, proj_back, near_send, near_recv, mid_send, mid_recv, far_send, far_recv,
+    count, hidden, proj_slots, back_grad, out_grad, gain, slot_row, qkv_term, proj_term, gathered,
+    block_out, conv_out, qkv_out, proj_out, gain_out,
+    grad_hidden, columns, proj_back,
+    near_send, near_recv, mid_send, mid_recv, far_send, far_recv,
+    mid_small, mid_small_in, far_small, far_small_in, small_sum,
     load, proj_sent, proj_got, near_sent, near_got, mid_sent, mid_got, far_sent, far_got,
 ):
     me = lax.axis_index("gx")
@@ -231,7 +236,7 @@
     proj_swap = Exchange(count, me, proj_slots, proj_back, proj_sent, proj_got)
     proj_swap.start()
 
-    picks = hot_columns(slot_col[...], back_grad.shape[0])
+    picks = hot_columns(slot_row[...], back_grad.shape[0])
     grad_back = dot(picks, back_grad[...])
     standard, inv_std = normalise(hidden[...])
     gain_term = jnp.sum(grad_back * standard, axis=0, keepdims=True)
@@ -245,9 +250,22 @@
             - standard * jnp.mean(scaled * standard, axis=-1, keepdims=True)
         )
     ).astype(BF16)
-    small_rows, channels = small.shape[1:]
-    at_row = lax.broadcasted_iota(jnp.int32, (small_rows, channels), 0)
-    gain_part = jnp.where(at_row == gain_row, 1.0, 0.0) * gain_term
+    each, channels = proj_term.shape[1:]
+    at_row = lax.broadcasted_iota(jnp.int32, (small_sum.shape[0] - 4 * each, channels), 0)
+    gain_part = jnp.where(at_row == 0, 1.0, 0.0) * gain_term
+
+    def put_small(target, base, mine, added=None):
+        def put(low, high, value):
+            target[base + low : base + high] = (
+                value if added is None else value + added[conv_rows + low : conv_rows + high]
+            )
+
+        for third in range(3):
+            block = qkv_term[mine, :, third * channels : (third + 1) * channels]
+            put(third * each, (third + 1) * each, block)
+        put(3 * each, 4 * each, proj_term[mine])
+        put(4 * each, small_sum.shape[0], gain_part)
+
     loading.wait()
 
     near = []
@@ -256,53 +274,63 @@
             place = 2 * step + part
             theirs = device(other, of_side, 1 - core)
             near_send[place, :conv_rows] = dot(columns[theirs], grad_hidden[...])
-            near_send[place, conv_rows:] = small[theirs] + gain_part
+            put_small(near_send.at[place], conv_rows, theirs)
             one = copy_to(near_send.at[place], near_recv.at[place], near_sent.at[place],
                           near_got.at[place], device(group, side, 1 - core))
             one.start()
             near.append(one)
 
-    def both_cores(place, mine):
+    def both_cores(place, mine, small):
         conv = dot(columns[mine], grad_hidden[...])
         near[place].wait_recv()
-        return (
-            conv + near_recv[place, :conv_rows],
-            small[mine] + gain_part + near_recv[place, conv_rows:],
-        )
-
-    mid = []
+        put_small(small, 0, mine, near_recv.at[place])
+        return conv + near_recv[place, :conv_rows]
+
+    mid, mid_f32 = [], []
     for step, other in enumerate(order):
-        conv, rest = both_cores(2 * step, device(other, 1 - side, core))
-        mid_send[step, :conv_rows] = conv.astype(BF16)
-        mid_send[step, conv_rows:] = rest.astype(BF16)
-        one = copy_to(mid_send.at[step], mid_recv.at[step], mid_sent.at[step], mid_got.at[step],
-                      device(group, 1 - side, core))
-        one.start()
-        mid.append(one)
-    far = []
+        conv = both_cores(2 * step, device(other, 1 - side, core), mid_small.at[step])
+        mid_send[step] = conv.astype(BF16)
+        peer = device(group, 1 - side, core)
+        mid.append(copy_to(mid_send.at[step], mid_recv.at[step], mid_sent.at[2 * step],
+                           mid_got.at[2 * step], peer))
+        mid_f32.append(copy_to(mid_small.at[step], mid_small_in.at[step],
+                               mid_sent.at[2 * step + 1], mid_got.at[2 * step + 1], peer))
+        mid[-1].start()
+        mid_f32[-1].start()
+    far, far_f32 = [], []
     for step, other in enumerate(order):
-        conv, rest = both_cores(2 * step + 1, device(other, side, core))
+        conv = both_cores(2 * step + 1, device(other, side, core), small_sum)
         mid[step].wait_recv()
-        conv += mid_recv[step, :conv_rows].astype(F32)
-        rest += mid_recv[step, conv_rows:].astype(F32)
+        mid_f32[step].wait_recv()
+        conv += mid_recv[step].astype(F32)
         if step < groups - 1:
-            far_send[step, :conv_rows] = conv.astype(BF16)
-            far_send[step, conv_rows:] = rest.astype(BF16)
-            one = copy_to(far_send.at[step], far_recv.at[step], far_sent.at[step],
-                          far_got.at[step], device(other, side, core))
-            one.start()
-            far.append(one)
+            far_send[step] = conv.astype(BF16)
+            far_small[step] = small_sum[...] + mid_small_in[step]
+            peer = device(other, side, core)
+            far.append(copy_to(far_send.at[step], far_recv.at[step], far_sent.at[2 * step],
+                               far_got.at[2 * step], peer))
+            far_f32.append(copy_to(far_small.at[step], far_small_in.at[step],
+                                   far_sent.at[2 * step + 1], far_got.at[2 * step + 1], peer))
+            far[-1].start()
+            far_f32[-1].start()
         else:
-            total_out[:conv_rows] = conv
-            total_out[conv_rows:] = rest
+            conv_out[...] = conv
+            small_sum[...] += mid_small_in[step]
     proj_swap.arrive()
     back_proj = dot(picks, proj_back[...].reshape(back_grad.shape))
     block_out[...] = (hidden[...] + back_proj).astype(BF16)
     for step in range(groups - 1):
         far[step].wait_recv()
-        total_out[...] += far_recv[step].astype(F32)
+        far_f32[step].wait_recv()
+        conv_out[...] += far_recv[step].astype(F32)
+        small_sum[...] += far_small_in[step]
+    for third in range(3):
+        block = small_sum[third * each : (third + 1) * each]
+        qkv_out[:, third * channels : (third + 1) * channels] = block
+    proj_out[...] = small_sum[3 * each : 4 * each]
+    gain_out[...] = small_sum[4 * each : 4 * each + 1]
     proj_swap.leave()
-    for one in near + mid + far:
+    for one in near + mid + mid_f32 + far + far_f32:
         one.wait_send()
 
 
@@ -333,8 +361,7 @@
     rim = rim_rows.shape[0] // 2
     kernel = neighbours.shape[0]
     gain = norm_gain.reshape(1, channels)
-    slot_row, slot_col = tile_slot.reshape(1, rows), tile_slot.reshape(rows, 1)
-    rows_row, rows_col = patch_rows.reshape(1, rows), patch_rows.reshape(rows, 1)
+    slot_row, rows_row = tile_slot.reshape(1, rows), patch_rows.reshape(1, rows)
 
     def full(*dims):
         return pl.BlockSpec(dims, lambda k: (0,) * len(dims))
@@ -357,8 +384,8 @@
         in_specs=[
             full(rows, channels),
             full(rows, channels),
-            full(2 * rim, 1),
-            pl.BlockSpec((each, 1, rows), lambda k: (k, 0, 0)),
+            full(1, 2 * rim),
+            full(kernel, rows),
             pl.BlockSpec((each, channels, channels), lambda k: (k, 0, 0)),
             full(1, channels),
             full(1, rows),
@@ -381,7 +408,7 @@
         compiler_params=params(collective_id=1, has_side_effects=True),
         name="conv",
     )(
-        features, out_grad, rim_rows.reshape(2 * rim, 1), neighbours.reshape(kernel, 1, rows),
+        features, out_grad, rim_rows.reshape(1, 2 * rim), neighbours,
         conv_weight.reshape(kernel, channels, channels), gain, slot_row,
     )
 
@@ -393,7 +420,7 @@
             shape((channels, 3 * channels), F32),
             shape((channels, channels), F32),
         ),
-        in_specs=[VMEM] * 6,
+        in_specs=[VMEM] * 5,
         out_specs=(VMEM, anywhere, VMEM, VMEM),
         scratch_shapes=[
             pltpu.VMEM((3 * channels, rows), BF16),
@@ -408,57 +435,59 @@
         name="attention",
     )(
         recv_normed.reshape(slots, channels), recv_grad.reshape(slots, channels),
-        rows_row, rows_col, qkv_weight, proj_weight,
+        rows_row, qkv_weight, proj_weight,
     )
 
     conv_rows = kernel * channels // count
     padded_rows = -(-conv_rows // 16) * 16
     one = channels // count
-    gain_row = 4 * one
-    small_rows = -(-(gain_row + 1) // 16) * 16
-    small = jnp.concatenate(
-        [
-            qkv_term.reshape(count, 3 * one, channels),
-            proj_term.reshape(count, one, channels),
-            jnp.zeros((count, small_rows - gain_row, channels), F32),
-        ],
-        axis=1,
-    )
+    small_rows = -(-(4 * one + 1) // 8) * 8
     columns = gathered.reshape(count, conv_rows, rows)
     if padded_rows > conv_rows:
         columns = jnp.pad(columns, ((0, 0), (0, padded_rows - conv_rows), (0, 0)))
     chips, groups, chunk = count // 2, count // 4, padded_rows + small_rows
-    block_out, total = pl.pallas_call(
-        functools.partial(backward_kernel, count, gain_row),
-        out_shape=(shape((rows, channels), BF16), shape((chunk, channels), F32)),
-        in_specs=[VMEM] * 7 + [anywhere],
-        out_specs=(VMEM, VMEM),
+    block_out, conv_grad, qkv_grad, proj_grad, gain_sum = pl.pallas_call(
+        functools.partial(backward_kernel, count),
+        out_shape=(
+            shape((rows, channels), BF16),
+            shape((padded_rows, channels), F32),
+            shape((one, 3 * channels), F32),
+            shape((one, channels), F32),
+            shape((1, channels), F32),
+        ),
+        in_specs=[VMEM] * 8 + [anywhere],
+        out_specs=(VMEM,) * 5,
         scratch_shapes=[
             pltpu.VMEM((rows, channels), BF16),
             pltpu.VMEM((count, padded_rows, rows), BF16),
             pltpu.VMEM(blocks, BF16),
             pltpu.VMEM((chips, chunk, channels), F32),
             pltpu.VMEM((chips, chunk, channels), F32),
-            pltpu.VMEM((groups, chunk, channels), BF16),
-            pltpu.VMEM((groups, chunk, channels), BF16),
-            pltpu.VMEM((groups - 1, chunk, channels), BF16),
-            pltpu.VMEM((groups - 1, chunk, channels), BF16),
+            pltpu.VMEM((groups, padded_rows, channels), BF16),
+            pltpu.VMEM((groups, padded_rows, channels), BF16),
+            pltpu.VMEM((groups - 1, padded_rows, channels), BF16),
+            pltpu.VMEM((groups - 1, padded_rows, channels), BF16),
+            pltpu.VMEM((groups, small_rows, channels), F32),
+            pltpu.VMEM((groups, small_rows, channels), F32),
+            pltpu.VMEM((groups - 1, small_rows, channels), F32),
+            pltpu.VMEM((groups - 1, small_rows, channels), F32),
+            pltpu.VMEM((small_rows, channels), F32),
             dma(1), dma(count), dma(count), dma(chips), dma(chips),
-            dma(groups), dma(groups), dma(groups), dma(groups),
+            dma(2 * groups), dma(2 * groups), dma(2 * groups), dma(2 * groups),
         ],
         compiler_params=params(collective_id=3, has_side_effects=True),
         name="backward",
     )(
         hidden, proj_slots.reshape(blocks), back_grad.reshape(slots, channels), out_grad, gain,
-        slot_col, small, columns,
-    )
-    small_sum = total[padded_rows:]
+        slot_row, qkv_term.reshape(count, one, 3 * channels),
+        proj_term.reshape(count, one, channels), columns,
+    )
     return (
         block_out,
-        total[:conv_rows],
-        small_sum[: 3 * one].reshape(one, 3 * channels),
-        small_sum[3 * one : gain_row],
-        lax.dynamic_slice_in_dim(small_sum[gain_row], lax.axis_index("gx") * one, one),
+        conv_grad[:conv_rows],
+        qkv_grad,
+        proj_grad,
+        lax.dynamic_slice_in_dim(gain_sum[0], lax.axis_index("gx") * one, one),
     )
 
 

time: 138 us -> 134 us (0.971); the launches traced: 137 us -> 131 us
  local copies, waits for them, and re-layouts: 12.6 us -> 7.41 us
    reshape x6 -> x0, local copies, waits for them, and re-layouts: 6.59 us -> none  [the longest x1 1.5 us: on_device(): neighbours.reshape(kernel, 1, rows)]
    unnamed x9 -> x4, local copies, waits for them, and re-layouts: 0.72 us -> 6.21 us
    slice x4 -> x0, local copies, waits for them, and re-layouts: 4.67 us -> none  [the longest x1 1.8 us: on_device(): total[:conv_rows]]
    pallas_call x1, Pallas kernels: 44.5 us -> 47.9 us  [on_device(): pl.pallas_call(functools.partial(backward_kernel, count), out_shape=(shap...]
    pallas_call x1, Pallas kernels: 41.1 us -> 39 us  [on_device(): pl.pallas_call(functools.partial(attention_kernel, count), out_shape=(sha...]
where the time goes in v3:
time: 134 us; the launch traced here: 131 us
  Pallas kernels  123 us (92%)
  local copies, waits for them, and re-layouts  7.41 us (6%)
    pallas_call x1, Pallas kernels, on_device(): pl.pallas_call(functools.partial(backward_kernel, count), out_shape=(shap...  47.9 us
    pallas_call x1, Pallas kernels, on_device(): pl.pallas_call(functools.partial(attention_kernel, count), out_shape=(sha...  39 us
    pallas_call x1, Pallas kernels, on_device(): pl.pallas_call(functools.partial(conv_kernel, count), grid=(kernel // eac...  36.3 us
    unnamed x4, local copies, waits for them, and re-layouts  6.21 us

profile of v3, /device:TPU:13, one launch (start us, length us, event | category | flops | bytes accessed | tf_op | source)
XLA Modules:
  0.0 131.4 jit_solution(1879841374467650003)
XLA Ops:
  0.6 36.3 %conv.1 = (bf16[27,256,512]{2,1,0:T(8,128)(2,1)}, f32[512,256]{1,0:T(8,128)}, bf16[16,64,256]{2,1,0:T(8,128)(2,1)}, bf16[16,64,256]{2,1,0:T(8,128)(2,1)}) custom-call(bf16[512,256]{1,0:T(8,128)(2,1)} %feats.1, bf16[512,256]{1,0:T(8,128)(2,1)} %out_grad.1, s32[1,128]{1,0:T(1,128)} %bitcast.27, s32[27,512]{1,0:T(8,128)} %nbrs.1, ...), custom_call_target="tpu_custom_call" | custom-call | tf_op jit(solution)/shard_map/conv/pallas_call | solution.py:375
  37.0 39.0 %attention.1 = (bf16[1024,256]{1,0:T(8,128)(2,1)}, bf16[16,64,256]{2,1,0:T(8,128)(2,1)}, f32[256,768]{1,0:T(8,128)}, f32[256,256]{1,0:T(8,128)}) custom-call(bf16[1024,256]{1,0:T(8,128)(2,1)} %bitcast.19, bf16[1024,256]{1,0:T(8,128)(2,1)} %bitcast.20, s32[1,512]{1,0:T(1,128)} %bitcast.26, bf16[256,768]{1,0:T(8,128)(2,1)} %qkv_w.1, bf16[256,256]{1,0:T(8,128)(2,1)} %proj_w.1), custom_call_target="tpu_custom_call" | custom-call | tf_op jit(solution)/shard_map/attention/pallas_call | solution.py:415
  76.0 47.9 %backward.1 = (bf16[512,256]{1,0:T(8,128)(2,1)}, f32[432,256]{1,0:T(8,128)}, f32[16,768]{1,0:T(8,128)}, f32[16,256]{1,0:T(8,128)}, f32[1,256]{1,0:T(1,128)}) custom-call(f32[512,256]{1,0:T(8,128)} %get-tuple-element.18.hidden, bf16[16,64,256]{2,1,0:T(8,128)(2,1)} %bitcast.17, bf16[1024,256]{1,0:T(8,128)(2,1)} %bitcast.18, bf16[512,256]{1,0:T(8,128)(2,1)} %out_grad.1, ...), custom_call_target="tpu_custom_call" | custom-call | tf_op jit(solution)/shard_map/backward/pallas_call | solution.py:449
  124.0 1.2 dynamic-slice_bitcast_fusion
  125.2 1.7 %copy.19 = bf16[512,256]{1,0:T(8,128)(2,1)} copy(bf16[512,256]{1,0:T(8,128)(2,1)} %get-tuple-element.36) | data formatting | bytes 524288
  126.8 1.8 %copy.20 = f32[432,256]{1,0:T(8,128)} copy(f32[432,256]{1,0:T(8,128)} %get-tuple-element.37) | data formatting | bytes 884736
  128.7 1.4 %copy.21 = f32[16,768]{1,0:T(8,128)} copy(f32[16,768]{1,0:T(8,128)} %get-tuple-element.38) | data formatting | bytes 98304
  130.1 1.3 %copy.22 = f32[16,256]{1,0:T(8,128)} copy(f32[16,256]{1,0:T(8,128)} %get-tuple-element.39) | data formatting | bytes 32768
